TPU v7x, 32 devices: a whole 2x2x4 slice. The times are simulated.
32 devices in a mesh: groups: 2 (over x), tensor: 16 (over z, y, core).
Axes of the slice: x: 2, y: 2, z: 4, core: 2. Of those that a mesh axis runs over, the one named last changes fastest.
Arguments:
- check_hidden_input: bfloat16 [2048, 8192], P('groups', 'tensor'), parts along dimension 0, may hold values from -6 to 6
- query_base_matrix: bfloat16 [16384, 8192], P(('groups', 'tensor')), parts along dimension 0, may hold values from -2 to 2
- adapter_input_factor: bfloat16 [16384, 32], P(('groups', 'tensor')), parts along dimension 0, may hold values from -0.1796875 to 0.1796875
- adapter_output_factor: bfloat16 [64, 8192], P('groups'), parts along dimension 0, may hold values from -1 to 1
- magnitude: float32 [16384], P('groups'), parts along dimension 0, may hold values from 0.5 to 4
- token_document_index: int32 [2048], P('groups'), parts along dimension 0, may hold values from 0 to 3, never falling along the last dimension, each value on 1 to 512 neighbouring positions
- keys: bfloat16 [2048, 1024], P('groups'), parts along dimension 0, may hold values from -300 to 300
- values: bfloat16 [2048, 1024], P('groups'), parts along dimension 0, may hold values from -6 to 6
Outputs:
- merged_weight: float32 [16384, 8192], P('groups', 'tensor'), parts along dimension 0
- attended: bfloat16 [2048, 8192], P('groups', 'tensor'), parts along dimension 0
There are 2 independent parts, one for each index of `groups`. A program takes and returns all parts, laid end to end along the dimension named above; each array names one. Nothing has to cross between parts.
Inputs may be any that keep to these rules, and one draw needn't show every extreme that they name: `token_document_index`: never falling; each document holds 1 to 512 tokens, one exactly 512.
All inputs are finite; a program needn't handle non-finite values.
Results may differ from a plain program's by a relative error of at most 0.0058.
Values may be sent and summed in bfloat16 or wider, within the bound.
No kernel may reach another device: no remote copies, remote signals or barrier semaphores. Data moves between devices by JAX's collectives and lax.ppermute only.
A program may use at most 128 MiB of HBM per device.

v0:
```python
import jax
import jax.numpy as jnp
from jax import lax
from jax.sharding import PartitionSpec as P

HD = 128
KVH = 8
GROUP = 8


def doc_positions(token_document_index):
    count = token_document_index.shape[0]
    index = jnp.arange(count, dtype=jnp.int32)
    starts = jnp.concatenate(
        [jnp.ones((1,), dtype=bool), token_document_index[1:] != token_document_index[:-1]]
    )
    first = lax.cummax(jnp.where(starts, index, jnp.int32(0)), axis=0)
    return (index - first).astype(jnp.float32)


def rotate(query, position):
    half = query.shape[-1] // 2
    freqs = 500000.0 ** (-(jnp.arange(half, dtype=jnp.float32) * 2.0 / query.shape[-1]))
    angle = position[:, None] * freqs[None, :]
    cosine = jnp.cos(angle)[:, None, :]
    sine = jnp.sin(angle)[:, None, :]
    first_half = query[..., :half]
    second_half = query[..., half:]
    return jnp.concatenate(
        [first_half * cosine - second_half * sine, second_half * cosine + first_half * sine],
        axis=-1,
    )


def attend_head(query_head, key_head, value_head, allowed):
    scores = jnp.dot(query_head, key_head.T, preferred_element_type=jnp.float32) / jnp.sqrt(
        jnp.float32(query_head.shape[-1])
    )
    scores = jnp.where(allowed, scores, -jnp.inf)
    top = jnp.max(scores, axis=1, keepdims=True)
    weights = jnp.exp(scores - top)
    probs = (weights / jnp.sum(weights, axis=1, keepdims=True)).astype(jnp.bfloat16)
    return jnp.dot(probs, value_head, preferred_element_type=jnp.float32).astype(jnp.bfloat16)


def shards(
    check_hidden_input,
    query_base_matrix,
    adapter_input_factor,
    adapter_output_factor,
    magnitude,
    token_document_index,
    keys,
    values,
):
    device_list = lax.axis_size("tensor")
    my_index = lax.axis_index("tensor")
    column_indices = adapter_output_factor.shape[1] // device_list
    updated_weight = query_base_matrix.astype(jnp.float32) + jnp.dot(
        adapter_input_factor, adapter_output_factor, preferred_element_type=jnp.float32
    )
    col_norm_sq = lax.psum(jnp.sum(updated_weight * updated_weight, axis=0), "tensor")
    scaled = updated_weight * (magnitude / jnp.sqrt(col_norm_sq + 1e-06))[None, :]
    merged_weight = lax.all_to_all(
        scaled.astype(jnp.bfloat16), "tensor", split_axis=1, concat_axis=0, tiled=True
    ).astype(scaled.dtype)
    serve_weight = merged_weight.astype(jnp.bfloat16)
    tokens = check_hidden_input.shape[0]
    query = jnp.dot(
        lax.all_gather(check_hidden_input, "tensor", axis=1, tiled=True),
        serve_weight,
        preferred_element_type=jnp.float32,
    )
    local_heads = column_indices // HD
    position = doc_positions(token_document_index)
    rotated = rotate(query.reshape(tokens, local_heads, HD), position).astype(jnp.bfloat16)
    index = jnp.arange(tokens, dtype=jnp.int32)
    allowed = (index[None, :] <= index[:, None]) & (
        token_document_index[None, :] == token_document_index[:, None]
    )
    key_heads = keys.reshape(tokens, KVH, HD)
    value_heads = values.reshape(tokens, KVH, HD)

    def one_head(local):
        kv_head = (my_index * local_heads + local) // GROUP
        query_head = lax.dynamic_index_in_dim(rotated, local, axis=1, keepdims=False)
        key_head = lax.dynamic_index_in_dim(key_heads, kv_head, axis=1, keepdims=False)
        value_head = lax.dynamic_index_in_dim(value_heads, kv_head, axis=1, keepdims=False)
        return attend_head(query_head, key_head, value_head, allowed)

    outputs = lax.map(one_head, jnp.arange(local_heads, dtype=jnp.int32))
    attended = jnp.transpose(outputs, (1, 0, 2)).reshape(tokens, column_indices)
    return (merged_weight, attended)


def solution(mesh):
    placed = (
        P("groups", "tensor"),
        P(("groups", "tensor"), None),
        P(("groups", "tensor"), None),
        P("groups", None),
        P("groups"),
        P("groups"),
        P("groups", None),
        P("groups", None),
    )
    return jax.shard_map(
        shards,
        mesh=mesh,
        in_specs=placed,
        out_specs=(P("groups", "tensor"), P("groups", "tensor")),
        check_vma=False,
    )
```

profile of v0, /device:TPU:13, one launch (start us, length us, event | category | flops | bytes accessed | tf_op | source)
XLA Modules:
  0.0 394.4 jit_solution(24340708069001138)
XLA Ops:
  7.2 0.0 copy-start
  7.2 0.0 all-gather.2.cloned.1.call-start
  7.2 0.7 all-gather.2.cloned.1.call-update
  7.9 0.3 copy-done
  8.2 0.0 copy-start.3
  8.2 9.7 %multiply_reduce_fusion = (f32[8192]{0:T(1024)S(1)}, f32[512,8192]{1,0:T(8,128)}) fusion(bf16[512,32]{0,1:T(8,128)(2,1)} %param.12, bf16[32,8192]{1,0:T(8,128)(2,1)S(1)} %copy-done, bf16[512,8192]{1,0:T(8,128)(2,1)} %param.11), kind=kOutput, calls=%fused_computation.20 | convolution fusion | flops 285204480 | bytes 25755648 | tf_op jit(solution)/shard_map/dot_general | solution.py:59
  17.9 63.3 %psum.7 = f32[8192]{0:T(1024)S(1)} all-reduce(f32[8192]{0:T(1024)S(1)} %get-tuple-element.166), channel_id=1, replica_groups=mesh['groups'=2,'tensor'=16] {'tensor'}, use_global_device_ids=true, to_apply=%region_1.0 | all-reduce | flops 8192 | bytes 65536 | tf_op jit(solution)/shard_map/psum | solution.py:62
  81.2 0.0 copy-done.3
  81.3 9.4 %multiply_convert_fusion = bf16[512,8192]{1,0:T(8,128)(2,1)} fusion(f32[512,8192]{1,0:T(8,128)} %get-tuple-element.167, f32[8192]{0:T(1024)S(1)} %rsqrt_multiply_fusion), kind=kLoop, calls=%fused_computation.19 | loop fusion | flops 8388608 | bytes 25198592 | tf_op jit(solution)/shard_map/convert_element_type | solution.py:65
  90.7 7.8 %copy.42 = bf16[64,16,8,512]{3,2,0,1:T(8,128)(2,1)} copy(bf16[64,16,8,512]{3,2,1,0:T(8,128)(2,1)} %bitcast.62) | data formatting | bytes 16777216 | tf_op jit(solution)/shard_map/all_to_all | solution.py:64
  98.5 0.0 copy-start.4
  98.5 0.0 copy-start.2
  98.5 6.3 %all-to-all-start = ((bf16[512,16,512]{2,0,1:T(8,128)(2,1)}), bf16[512,16,512]{2,0,1:T(8,128)(2,1)}, u32[]{:S(2)}, u32[]{:S(2)}) async-start(bf16[512,16,512]{2,0,1:T(8,128)(2,1)} %bitcast.61), calls=%async_computation | async-start | bytes 16777216 | tf_op jit(solution)/shard_map/all_to_all | solution.py:64
  104.7 0.0 copy-done.4
  104.7 0.1 slice_compare_fusion
  104.8 0.1 add_select_fusion
  104.9 0.3 reduce-window.9
  105.2 0.1 slice.22
  105.3 0.0 copy-done.2
  105.3 2.6 copy.29
  107.9 3.9 %copy.30 = bf16[1024,1024]{0,1:T(8,128)(2,1)} copy(bf16[1024,1024]{1,0:T(8,128)(2,1)} %param.17) | data formatting | bytes 4194304 | tf_op args[7]
  111.9 0.1 slice_reduce_fusion
  112.0 0.1 fusion.16
  112.1 1.9 multiply_cosine_fusion
  113.9 202.2 %all-to-all-done = bf16[512,16,512]{2,0,1:T(8,128)(2,1)} async-done(((bf16[512,16,512]{2,0,1:T(8,128)(2,1)}), bf16[512,16,512]{2,0,1:T(8,128)(2,1)}, u32[]{:S(2)}, u32[]{:S(2)}) %all-to-all-start) | async-done | bytes 8388640 | tf_op jit(solution)/shard_map/all_to_all | solution.py:64
  316.1 12.0 %bitcast_convert_fusion = f32[8192,512]{1,0:T(8,128)} fusion(bf16[512,16,512]{2,0,1:T(8,128)(2,1)} %all-to-all-done), kind=kLoop, calls=%fused_computation.37 | loop fusion | flops 4194304 | bytes 25165824 | tf_op jit(solution)/shard_map/convert_element_type | solution.py:66
  328.1 0.0 all-gather.2.cloned.1.call-done
  328.1 14.4 %fusion.19 = f32[512,1024]{1,0:T(8,128)S(1)} fusion(bf16[8192,512]{1,0:T(8,128)(2,1)} %bitcast.1, bf16[1024,8192]{1,0:T(8,128)(2,1)} %all-gather.2.cloned.1.call-done), kind=kOutput, calls=%fused_computation.40 | convolution fusion | flops 8589934592 | bytes 27262976 | tf_op jit(solution)/shard_map/dot_general | solution.py:69
  342.5 1.6 fusion.18
  344.1 1.8 copy.36
  345.9 3.2 copy.37
  349.1 2.1 subtract_convert_fusion
  351.3 0.6 pad_maximum_fusion
  351.9 33.3 %while.13 = (s32[]{:T(128)}, bf16[4,1024,128]{2,1,0:T(8,128)(2,1)}, s32[4]{0:T(128)S(1)}, bf16[1024,4,128]{2,0,1:T(8,128)(2,1)S(1)}, s32[]{:T(128)}, /*index=5*/...) while((s32[]{:T(128)}, bf16[4,1024,128]{2,1,0:T(8,128)(2,1)}, ...), condition=%wide.region_7.8_spmd.clone, body=%wide.region_4.7_spmd.clone.sunk | while | flops 548534272 | bytes 13661067 | solution.py:91
  351.9 0.6 dynamic_slice.54
  355.1 1.9 fusion.30
  357.0 0.6 fusion.31
  357.6 2.6 fusion.32
  360.2 0.6 dynamic_slice.54
  363.4 1.9 fusion.30
  365.3 0.6 fusion.31
  366.0 2.6 fusion.32
  368.5 0.6 dynamic_slice.54
  371.7 1.9 fusion.30
  373.7 0.6 fusion.31
  374.3 2.6 fusion.32
  376.9 0.6 dynamic_slice.54
  380.1 1.9 fusion.30
  382.0 0.6 fusion.31
  382.6 2.6 fusion.32
  385.2 0.0 copy-start.1
  385.2 2.4 copy_bitcast_fusion.1
  387.6 0.0 copy-done.1
  (5 shorter events, 0.1 us)
Async XLA Ops:
  7.2 1.1 copy-start
  7.2 320.9 %all-gather.2.cloned.1.call-start = ((), (), s32[]{:S(2)}) async-start(), calls=%async_computation.1 | async-start | bytes 17825792 | tf_op jit(solution)/shard_map/all_gather | solution.py:70
  8.2 73.0 %copy-start.3 = (f32[8192]{0:T(1024)S(1)}, f32[8192]{0:T(1024)}, u32[]{:S(2)}) copy-start(f32[8192]{0:T(1024)} %param.14) | copy-start | bytes 98308
  98.5 6.3 %copy-start.4 = (s32[1024]{0:T(1024)S(1)}, s32[1024]{0:T(1024)}, u32[]{:S(2)}) copy-start(s32[1024]{0:T(1024)} %param.15) | copy-start | bytes 12292
  98.5 6.8 %copy-start.2 = (bf16[1024,1024]{1,0:T(8,128)(2,1)S(1)}, bf16[1024,1024]{1,0:T(8,128)(2,1)}, u32[]{:S(2)}) copy-start(bf16[1024,1024]{1,0:T(8,128)(2,1)} %param.16) | copy-start | bytes 6291460
  98.5 217.7 %all-to-all-start = ((bf16[512,16,512]{2,0,1:T(8,128)(2,1)}), bf16[512,16,512]{2,0,1:T(8,128)(2,1)}, u32[]{:S(2)}, u32[]{:S(2)}) async-start(bf16[512,16,512]{2,0,1:T(8,128)(2,1)} %bitcast.61), calls=%async_computation | async-start | bytes 16777216 | tf_op jit(solution)/shard_map/all_to_all | solution.py:64
  385.2 2.4 copy-start.1
Sparse Core Ops, SparseCore 0:
  10.2 183.7 all-gather.1
where the time goes:
time: 395 us; the launch traced here: 394 us
  waiting for transfers between devices  203 us (51%)
  blocking collectives  63.3 us (16%)
  matrix products  42.2 us (11%)
  other arithmetic  29 us (7%)
  local copies, waits for them, and re-layouts  26.1 us (7%)
  between operations  14.1 us (4%)
  loops' own time  10.5 us (3%)
  starting transfers between devices  6.3 us (2%)
    all_to_all x1, waiting for transfers between devices, shards(): lax.all_to_all(scaled.astype(jnp.bfloat16), 'tensor', split_axis=1, conca...  202 us
    psum x1, blocking collectives, shards(): lax.psum(jnp.sum(updated_weight * updated_weight, axis=0), 'tensor')  63.3 us
    dot_general x1, matrix products, shards(): jnp.dot(lax.all_gather(check_hidden_input, 'tensor', axis=1, tiled=True),...  14.4 us
    convert_element_type x1, other arithmetic, shards(): merged_weight = lax.all_to_all(scaled.astype(jnp.bfloat16), 'tensor', spl...  12 us
    unnamed x14, local copies, waits for them, and re-layouts  11.9 us
    another operation x1, loops' own time, shards(): outputs = lax.map(one_head, jnp.arange(local_heads, dtype=jnp.int32))  10.5 us
    dot_general x4, matrix products, attend_head(): jnp.dot(probs, value_head, preferred_element_type=jnp.float32)  10.3 us
    dot_general x1, matrix products, shards(): jnp.dot(adapter_input_factor, adapter_output_factor, preferred_element_ty...  9.71 us
  transfers between devices with their start and end apart: 2, of which 1 were waited for; matrix products, arithmetic and copies ran while one was open for 12% of the time, Pallas kernels for 0%

commit v1 on v0

v1 whole, which is shorter than its diff:
```python
import functools

import jax
import jax.numpy as jnp
from jax import lax
from jax.experimental import pallas as pl
from jax.experimental.pallas import tpu as pltpu
from jax.sharding import PartitionSpec as P

HD = 128
KVH = 8
GROUP = 8
DOC_MAX = 512
Q_BLOCK = 256


def doc_positions(token_document_index):
    count = token_document_index.shape[0]
    index = jnp.arange(count, dtype=jnp.int32)
    starts = jnp.concatenate(
        [jnp.ones((1,), dtype=bool), token_document_index[1:] != token_document_index[:-1]]
    )
    first = lax.cummax(jnp.where(starts, index, jnp.int32(0)), axis=0)
    return (index - first).astype(jnp.float32)


def rope_tables(position):
    half = HD // 2
    freqs = 500000.0 ** (-(jnp.arange(half, dtype=jnp.float32) * 2.0 / HD))
    angle = position[:, None] * freqs[None, :]
    cosine = jnp.cos(angle)
    sine = jnp.sin(angle)
    return jnp.concatenate([cosine, cosine], axis=1), jnp.concatenate([-sine, sine], axis=1)


def cut_kernel(me_ref, a_ref, b_ref, w_ref, *refs):
    outs, sums_ref, (stage, in_sem, out_sem) = refs[:-4], refs[-4], refs[-3:]
    me = me_ref[0]
    n, _, width = stage.shape

    def column(e):
        return pl.multiple_of((me ^ e) * width, width)

    order = (8, 12, 9, 13, 4, 10, 14, 5, 11, 15, 6, 7, 2, 3, 1, 0)
    reads = {
        e: pltpu.make_async_copy(w_ref.at[:, pl.ds(column(e), width)], stage.at[e], in_sem.at[e])
        for e in order
    }
    writes = {e: pltpu.make_async_copy(stage.at[e], outs[e], out_sem.at[e]) for e in order}
    for e in order:
        reads[e].start()
    for e in order:
        reads[e].wait()
        writes[e].start()
        updated = stage[e].astype(jnp.float32) + jnp.dot(
            a_ref[...], b_ref[:, pl.ds(column(e), width)], preferred_element_type=jnp.float32
        )
        part = jnp.sum((updated * updated).reshape(-1, 8, width), axis=0)
        sums_ref[pl.ds(e, 1), :] = jnp.sum(part, axis=0, keepdims=True)
    for e in order:
        writes[e].wait()


def cut(me, a, b, w):
    rows, width = w.shape[0], w.shape[1] // 16
    vmem, hbm = pl.BlockSpec(memory_space=pltpu.VMEM), pl.BlockSpec(memory_space=pl.ANY)
    *blocks, sums = pl.pallas_call(
        cut_kernel,
        out_shape=[jax.ShapeDtypeStruct((rows, width), w.dtype)] * 16
        + [jax.ShapeDtypeStruct((16, width), jnp.float32)],
        in_specs=[pl.BlockSpec(memory_space=pltpu.SMEM), vmem, vmem, hbm],
        out_specs=[hbm] * 16 + [vmem],
        scratch_shapes=[
            pltpu.VMEM((16, rows, width), w.dtype),
            pltpu.SemaphoreType.DMA((16,)),
            pltpu.SemaphoreType.DMA((16,)),
        ],
        compiler_params=pltpu.CompilerParams(vmem_limit_bytes=24 * 1024 * 1024),
        cost_estimate=pl.CostEstimate(
            flops=4 * w.size, bytes_accessed=4 * w.size, transcendentals=0
        ),
    )(me, a, b, w)
    return blocks, sums


def merge_kernel(plan, me_ref, b_ref, mag_ref, total_ref, *refs):
    (slots, xor, rows, w_at, x_at, n_w, n_x, local, first, last) = plan
    w_refs, refs = refs[:n_w], refs[n_w:]
    x_refs, refs = refs[:n_x], refs[n_x:]
    if last:
        (cos_ref, sin_ref, row_ref, col_ref, k_ref, v_ref), refs = refs[:6], refs[6:]
    if not first:
        (q_in, _), refs = refs[:2], refs[2:]
    (merged_ref, q_out), refs = refs[:2], refs[2:]
    (w_buf, x_buf, a_buf, u_buf, w_sem, x_sem, a_sem, m_sem), refs = refs[:8], refs[8:]
    if last:
        q_buf, k_buf, v_buf, k_sem, q_sem, o_sem = refs
    else:
        q_buf = q_out
    tokens = x_buf.shape[1]
    me = me_ref[0]
    count = len(slots)

    def part(refs, spot):
        which, index = spot
        return refs[which] if index is None else refs[which].at[index]

    def w_copy(k):
        return pltpu.make_async_copy(part(w_refs, w_at[k]), w_buf.at[k], w_sem.at[k])

    def x_copy(k):
        src = part(x_refs, x_at[k]).at[pl.ds(0, tokens)]
        return pltpu.make_async_copy(src, x_buf.at[k], x_sem.at[k])

    def a_copy(k):
        src = part(x_refs, x_at[k]).at[pl.ds(tokens, a_buf.shape[1])]
        return pltpu.make_async_copy(src, a_buf.at[k], a_sem.at[k])

    def out_copy(k):
        row = pl.multiple_of(((me ^ slots[k]) if xor else slots[k]) * rows, rows)
        return pltpu.make_async_copy(u_buf.at[k], merged_ref.at[pl.ds(row, rows), :], m_sem.at[k])

    for k in range(count):
        w_copy(k).start()
        a_copy(k).start()
        x_copy(k).start()
    if last:
        column = pl.multiple_of(me * local // GROUP * HD, HD)
        kv_copies = [
            pltpu.make_async_copy(ref.at[:, pl.ds(column, HD)], buf, k_sem.at[j])
            for j, (ref, buf) in enumerate(((k_ref, k_buf), (v_ref, v_buf)))
        ]
        for copy in kv_copies:
            copy.start()
        if not first:
            q_copy = pltpu.make_async_copy(q_in, q_buf, q_sem)
            q_copy.start()

    scale = mag_ref[...] / jnp.sqrt(total_ref[...] + 1e-06)
    for k in range(count):
        w_copy(k).wait()
        a_copy(k).wait()
        updated = w_buf[k].astype(jnp.float32) + lax.dot_general(
            a_buf[k], b_ref[...], (((0,), (0,)), ((), ())), preferred_element_type=jnp.float32
        )
        merged = updated * scale
        u_buf[k] = merged
        out_copy(k).start()
        x_copy(k).wait()
        product = jnp.dot(x_buf[k], merged.astype(jnp.bfloat16), preferred_element_type=jnp.float32)
        if k == 0 and first:
            q_buf[...] = product
        elif k == 0 and not last:
            q_buf[...] = q_in[...] + product
        else:
            if k == 0:
                q_copy.wait()
            q_buf[...] += product

    if last:
        for copy in kv_copies:
            copy.wait()
        attend(q_buf, cos_ref, sin_ref, row_ref, col_ref, k_buf, v_buf, q_out, local)
    for k in range(count):
        out_copy(k).wait()


def attend(q_ref, cos_ref, sin_ref, row_ref, col_ref, k_ref, v_ref, att_ref, local):
    tokens = q_ref.shape[0]
    for t in range(0, tokens, Q_BLOCK):
        low, high = max(0, t - DOC_MAX), t + Q_BLOCK
        shape = (Q_BLOCK, high - low)
        later = lax.broadcasted_iota(jnp.int32, shape, 0) + (t - low)
        allowed = (lax.broadcasted_iota(jnp.int32, shape, 1) <= later) & (
            row_ref[:, pl.ds(low, high - low)] == col_ref[pl.ds(t, Q_BLOCK), :]
        )
        cosine, sine = cos_ref[pl.ds(t, Q_BLOCK), :], sin_ref[pl.ds(t, Q_BLOCK), :]
        for h in range(local):
            lanes = pl.ds(h * HD, HD)
            query = q_ref[pl.ds(t, Q_BLOCK), lanes]
            turned = pltpu.roll(query, HD // 2, 1)
            rotated = (query * cosine + turned * sine).astype(jnp.bfloat16)
            scores = lax.dot_general(
                rotated,
                k_ref[pl.ds(low, high - low), :],
                (((1,), (1,)), ((), ())),
                preferred_element_type=jnp.float32,
            ) * jnp.float32(HD**-0.5)
            scores = jnp.where(allowed, scores, -jnp.inf)
            top = jnp.max(scores, axis=1, keepdims=True)
            weights = jnp.exp(scores - top)
            probs = (weights / jnp.sum(weights, axis=1, keepdims=True)).astype(jnp.bfloat16)
            att_ref[pl.ds(t, Q_BLOCK), lanes] = jnp.dot(
                probs, v_ref[pl.ds(low, high - low), :], preferred_element_type=jnp.float32
            ).astype(jnp.bfloat16)


def merge(me, b, mag, total, slots, w_list, w_at, x_list, x_at, sizes, xor, previous=None, attention=None):
    features, rows, tokens, rank = sizes
    width, count = b.shape[1], len(slots)
    first, last = previous is None, attention is not None
    plan = (slots, xor, rows, w_at, x_at, len(w_list), len(x_list), width // HD, first, last)
    vmem, hbm = pl.BlockSpec(memory_space=pltpu.VMEM), pl.BlockSpec(memory_space=pl.ANY)
    operands = [me, b, mag, total, *w_list, *x_list]
    in_specs = [pl.BlockSpec(memory_space=pltpu.SMEM)] + [vmem] * 3 + [hbm] * (len(w_list) + len(x_list))
    scratch = [
        pltpu.VMEM((count, rows, width), jnp.bfloat16),
        pltpu.VMEM((count, tokens, rows), jnp.bfloat16),
        pltpu.VMEM((count, rank, rows), jnp.bfloat16),
        pltpu.VMEM((count, rows, width), jnp.float32),
    ] + [pltpu.SemaphoreType.DMA((count,))] * 4
    if last:
        operands += list(attention)
        in_specs += [vmem] * 4 + [hbm] * 2
        scratch += [
            pltpu.VMEM((tokens, width), jnp.float32),
            pltpu.VMEM((tokens, HD), jnp.bfloat16),
            pltpu.VMEM((tokens, HD), jnp.bfloat16),
            pltpu.SemaphoreType.DMA((2,)),
            pltpu.SemaphoreType.DMA,
            pltpu.SemaphoreType.DMA,
        ]
    aliases = {}
    if not first:
        merged, query = previous
        operands += [query, merged]
        in_specs += [hbm if last else vmem, hbm]
        aliases = {len(operands) - 1: 0}
    return pl.pallas_call(
        functools.partial(merge_kernel, plan),
        out_shape=[
            jax.ShapeDtypeStruct((features, width), jnp.float32),
            jax.ShapeDtypeStruct((tokens, width), jnp.bfloat16 if last else jnp.float32),
        ],
        in_specs=in_specs,
        out_specs=[hbm, vmem],
        scratch_shapes=scratch,
        input_output_aliases=aliases,
        compiler_params=pltpu.CompilerParams(vmem_limit_bytes=48 * 1024 * 1024),
        cost_estimate=pl.CostEstimate(
            flops=2 * tokens * count * rows * width,
            bytes_accessed=count * rows * (6 * width + 2 * tokens),
            transcendentals=width // HD * tokens * tokens if last else 0,
        ),
    )(*operands)


def after(array, others):
    if not others:
        return array
    return lax.optimization_barrier((array, *others))[0]


ROUNDS = (
    ("z2", "z1", "y0", "s1", "w2", "s2", "s4"),
    ("z3", "y1", "y2", "w8", "w12"),
    ("y3", "cA", "w9", "w13", "w4"),
    ("cD", "w10", "w14", "w5", "w3", "s8"),
    ("w11", "w15", "w6", "w7", "w1"),
)
LINES = {"z1": ("x", 4), "z2": ("x", 8), "z3": ("z2", 4), "y0": ("x", 2), "y1": ("z1", 2), "y2": ("z2", 2), "y3": ("z3", 2)}
STACKS = {"cA": ("x", "z1", "z2", "y0"), "cD": ("z3", "y1", "y2", "y3")}
GROUPS = ((0, 8, 12, 4, 9, 2), (13, 10, 14, 5, 3), (6, 7, 1), (11, 15))


def exchange(x, blocks, sums):
    def swap(array, d):
        return lax.ppermute(array, "tensor", [(i, i ^ d) for i in range(16)])

    got = {"x": x}
    partial = sums.reshape(8, 2, -1)

    def payload(name):
        if name in LINES:
            return got[LINES[name][0]], LINES[name][1]
        if name in STACKS:
            return jnp.stack([got[k] for k in STACKS[name]]), 1
        d = int(name[1:])
        return (partial[:, 1] if name[0] == "s" else blocks[d]), d

    def heavy(name):
        return name[0] == "w"

    for k, names in enumerate(ROUNDS):
        new = {}
        for name in names:
            gates = [m for m in ROUNDS[k - 1] if not (heavy(name) and heavy(m))] if k else []
            gates += ROUNDS[k - 2] if k > 1 else ()
            array, d = payload(name)
            new[name] = swap(after(array, [got[m] for m in gates]), d)
            if name[0] == "s":
                partial = partial[:, 0] + new[name]
                if d < 8:
                    partial = partial.reshape(4 // d, 2, -1)
        got.update(new)
    x_list = [got[k] for k in ("x", "z1", "z2", "z3", "y0", "y1", "y2", "y3", "cA", "cD")]
    x_at = [None] * 16
    for k, d in enumerate((0, 4, 8, 12, 2, 6, 10, 14)):
        x_at[d] = (k, None)
    for k, d in enumerate((1, 5, 9, 3)):
        x_at[d] = (8, k)
    for k, d in enumerate((13, 7, 11, 15)):
        x_at[d] = (9, k)
    weights = [blocks[0]] + [got["w" + str(d)] for d in range(1, 16)]
    return x_list, x_at, weights, partial


def shards(
    check_hidden_input,
    query_base_matrix,
    adapter_input_factor,
    adapter_output_factor,
    magnitude,
    token_document_index,
    keys,
    values,
):
    n = lax.axis_size("tensor")
    my_index = lax.axis_index("tensor")
    rows, features = query_base_matrix.shape
    tokens, rank = check_hidden_input.shape[0], adapter_output_factor.shape[0]
    width = features // n
    me = my_index.astype(jnp.int32).reshape(1)
    b = lax.dynamic_slice_in_dim(adapter_output_factor, my_index * width, width, axis=1)
    mag = lax.dynamic_slice_in_dim(magnitude, my_index * width, width, axis=0)[None, :]
    cosine, sine = rope_tables(doc_positions(token_document_index))
    x = jnp.concatenate([check_hidden_input, adapter_input_factor.T], axis=0)
    attention = (cosine, sine, token_document_index[None, :], token_document_index[:, None], keys, values)
    sizes = (n * rows, rows, tokens, rank)
    if n == 16:
        blocks, sums = cut(me, adapter_input_factor, adapter_output_factor, query_base_matrix)
        x_list, x_at, weights, total = exchange(x, blocks, sums)
        done = None
        for k, slots in enumerate(GROUPS):
            used = sorted({x_at[d][0] for d in slots})
            done = merge(
                me, b, mag, total, slots,
                [weights[d] for d in slots], [(j, None) for j in range(len(slots))],
                [x_list[j] for j in used], [(used.index(x_at[d][0]), x_at[d][1]) for d in slots],
                sizes, True, done, attention if k == len(GROUPS) - 1 else None,
            )
        return done[0], done[1]
    x_all = lax.all_gather(x, "tensor", axis=0)
    w_cut = jnp.transpose(query_base_matrix.reshape(rows, n, width), (1, 0, 2))
    w_all = lax.all_to_all(w_cut, "tensor", split_axis=0, concat_axis=0, tiled=True)
    low_rank = lax.dot_general(x_all[:, tokens:], b, (((1,), (0,)), ((), ())), preferred_element_type=jnp.float32)
    total = jnp.sum(jnp.square(w_all.astype(jnp.float32) + low_rank), axis=(0, 1))[None, :]
    slots = tuple(range(n))
    at = [(0, d) for d in slots]
    merged, attended = merge(me, b, mag, total, slots, [w_all], at, [x_all], at, sizes, False, None, attention)
    return merged, attended


def solution(mesh):
    placed = (
        P("groups", "tensor"),
        P(("groups", "tensor"), None),
        P(("groups", "tensor"), None),
        P("groups", None),
        P("groups"),
        P("groups"),
        P("groups", None),
        P("groups", None),
    )
    return jax.shard_map(
        shards,
        mesh=mesh,
        in_specs=placed,
        out_specs=(P("groups", "tensor"), P("groups", "tensor")),
        check_vma=False,
    )
```

time: 395 us -> 280 us (0.71)
  the two profiles are of different devices: /device:TPU:13 before, /device:TPU:0 now
where the time goes in v1:
time: 280 us; the launch traced here: 279 us
  waiting for transfers between devices  150 us (54%)
  Pallas kernels  43.7 us (16%)
  starting transfers between devices  41.4 us (15%)
  local copies, waits for them, and re-layouts  29.8 us (11%)
  other arithmetic  12.7 us (5%)
    ppermute x28, waiting for transfers between devices, swap(): return lax.ppermute(array, 'tensor', [(i, i ^ d) for i in range(16)])  150 us
    ppermute x28, starting transfers between devices, swap(): return lax.ppermute(array, 'tensor', [(i, i ^ d) for i in range(16)])  41.4 us
    pallas_call x4, Pallas kernels, merge(): pl.pallas_call(functools.partial(merge_kernel, plan), out_shape=[jax.Shap...  37 us
    unnamed x92, local copies, waits for them, and re-layouts  26.7 us
    another operation x3, other arithmetic, payload(): return (jnp.stack([got[k] for k in STACKS[name]]), 1)  7.04 us
    pallas_call x1, Pallas kernels, cut(): pl.pallas_call(cut_kernel, out_shape=[jax.ShapeDtypeStruct((rows, width),...  6.71 us
  transfers between devices with their start and end apart: 28, of which 13 were waited for; matrix products, arithmetic and copies ran while one was open for 5% of the time, Pallas kernels for 11%

profile of v1, /device:TPU:0, one launch (start us, length us, event | category | flops | bytes accessed | tf_op | source)
XLA Modules:
  0.0 279.1 jit_solution(15687173089442510382)
XLA Ops:
  0.6 2.4 fusion.7
  3.0 4.0 %collective-permute-start.3 = (bf16[1056,512]{1,0:T(8,128)(2,1)S(1)}, bf16[1056,512]{1,0:T(8,128)(2,1)}, u32[]{:S(2)}, u32[]{:S(2)}) collective-permute-start(bf16[1056,512]{1,0:T(8,128)(2,1)S(1)} %get-tuple-element.89.refs_6_), channel_id=1, source_target_pairs={{0,8},{1,9},{2,10},{3,11},{4,12},{5,13},{6,14},{7,15},{8,0},{9,1},... | collective-permute-start | bytes 3244040 | tf_op jit(solution)/shard_map/ppermute | solution.py:268
  7.1 1.6 collective-permute-start.4
  8.6 1.5 collective-permute-start.5
  10.3 3.4 %copy-done = bf16[512,8192]{1,0:T(8,128)(2,1)S(1)} copy-done((bf16[512,8192]{1,0:T(8,128)(2,1)S(1)}, bf16[512,8192]{1,0:T(8,128)(2,1)}, u32[]{:S(2)}) %copy-start) | copy-done | bytes 8388632
  13.7 1.0 copy-done.8
  14.7 6.7 %shard_map.95 = (bf16[512,512]{1,0:T(8,128)(2,1)S(1)}, bf16[512,512]{1,0:T(8,128)(2,1)S(1)}, bf16[512,512]{1,0:T(8,128)(2,1)S(1)}, bf16[512,512]{1,0:T(8,128)(2,...) custom-call(s32[1]{0:T(128)} %bitcast.me_ref, ...), custom_call_target="tpu_custom_call" | custom-call | flops 16777216 | bytes 16777216 | tf_op jit(solution)/shard_map/pallas_call | solution.py:67
  21.4 0.8 copy-done.11
  22.2 0.8 copy-done.24
  23.0 0.8 copy-done.25
  23.9 0.8 copy-done.26
  24.7 0.8 copy-done.27
  25.5 0.8 copy-done.28
  26.3 0.8 copy-done.29
  27.1 0.8 copy-done.30
  27.9 0.8 copy-done.31
  29.5 0.8 copy-done.33
  30.3 0.8 copy-done.35
  31.1 0.8 copy-done.37
  31.9 0.8 copy-done.39
  32.7 0.8 copy-done.40
  33.4 0.8 copy-done.41
  35.6 1.0 collective-permute-start.1
  36.6 12.5 %collective-permute-done.1 = f32[4,512]{1,0:T(4,128)S(1)} collective-permute-done((f32[4,512]{1,0:T(4,128)S(1)}, f32[4,512]{1,0:T(4,128)S(1)}, u32[]{:S(2)}, u32[]{:S(2)}) %collective-permute-start.1) | collective-permute-done | bytes 8224 | tf_op jit(solution)/shard_map/ppermute | solution.py:268
  49.7 4.8 %collective-permute-done.2 = f32[2,512]{1,0:T(2,128)S(1)} collective-permute-done((f32[2,512]{1,0:T(2,128)S(1)}, f32[2,512]{1,0:T(2,128)S(1)}, u32[]{:S(2)}, u32[]{:S(2)}) %collective-permute-start.2) | collective-permute-done | bytes 4128 | tf_op jit(solution)/shard_map/ppermute | solution.py:268
  54.5 0.8 copy-done.13
  55.3 1.6 collective-permute-start.8
  56.9 1.4 collective-permute-start.7
  58.9 1.4 collective-permute-start.11
  60.9 2.3 pad_maximum_fusion
  63.2 32.8 %collective-permute-done.11.refs_2_ = bf16[512,512]{1,0:T(8,128)(2,1)S(1)} collective-permute-done((bf16[512,512]{1,0:T(8,128)(2,1)}, bf16[512,512]{1,0:T(8,128)(2,1)S(1)}, u32[]{:S(2)}, u32[]{:S(2)}) %collective-permute-start.11) | collective-permute-done | bytes 524320 | tf_op jit(solution)/shard_map/ppermute | solution.py:268
  96.0 0.8 copy-done.15
  96.8 6.4 %collective-permute-done.10.refs_1_ = bf16[512,512]{1,0:T(8,128)(2,1)S(1)} collective-permute-done((bf16[512,512]{1,0:T(8,128)(2,1)}, bf16[512,512]{1,0:T(8,128)(2,1)S(1)}, u32[]{:S(2)}, u32[]{:S(2)}) %collective-permute-start.10) | collective-permute-done | bytes 524320 | tf_op jit(solution)/shard_map/ppermute | solution.py:268
  103.2 0.8 copy-done.17
  104.0 1.1 collective-permute-done.7.refs_9_
  105.1 3.2 %collective-permute-start.12 = (bf16[1056,512]{1,0:T(8,128)(2,1)S(1)}, bf16[1056,512]{1,0:T(8,128)(2,1)S(1)}, u32[]{:S(2)}, u32[]{:S(2)}) collective-permute-start(bf16[1056,512]{1,0:T(8,128)(2,1)S(1)} %collective-permute-done.7.refs_9_), channel_id=1, source_target_pairs={{0,2},{1,3},{2,0},{3,1},{4,6},{5,7},{6,4},{7,5},{8,10},{9,11},{10,... | collective-permute-start | bytes 3244040 | tf_op jit(solution)/shard_map/ppermute | solution.py:268
  108.3 2.2 collective-permute-start.15
  110.6 1.0 collective-permute-start.14
  111.5 21.2 %collective-permute-done.12.refs_6_ = bf16[1056,512]{1,0:T(8,128)(2,1)S(1)} collective-permute-done((bf16[1056,512]{1,0:T(8,128)(2,1)S(1)}, bf16[1056,512]{1,0:T(8,128)(2,1)S(1)}, u32[]{:S(2)}, u32[]{:S(2)}) %collective-permute-start.12) | collective-permute-done | bytes 1081376 | tf_op jit(solution)/shard_map/ppermute | solution.py:268
  132.8 2.4 pad_maximum_fusion.1
  135.2 0.8 copy-done.19
  136.0 0.8 copy-done.9
  136.9 20.8 %collective-permute-done.14.refs_4_ = bf16[512,512]{1,0:T(8,128)(2,1)S(1)} collective-permute-done((bf16[512,512]{1,0:T(8,128)(2,1)S(1)}, bf16[512,512]{1,0:T(8,128)(2,1)S(1)}, u32[]{:S(2)}, u32[]{:S(2)}) %collective-permute-start.14) | collective-permute-done | bytes 524320 | tf_op jit(solution)/shard_map/ppermute | solution.py:268
  157.7 0.9 copy-done.21
  159.6 3.1 %collective-permute-start.26 = (bf16[512,512]{1,0:T(8,128)(2,1)}, bf16[512,512]{1,0:T(8,128)(2,1)}, u32[]{:S(2)}, u32[]{:S(2)}) collective-permute-start(bf16[512,512]{1,0:T(8,128)(2,1)} %copy-done.31), channel_id=1, source_target_pairs={{0,5},{1,4},{2,7},{3,6},{4,1},{5,0},{6,3},{7,2},{8,13},{9,12},{10,... | collective-permute-start | bytes 1572872 | tf_op jit(solution)/shard_map/ppermute | solution.py:268
  162.7 2.4 collective-permute-start.25
  165.1 3.2 %fusion = (f32[1024,64]{1,0:T(8,128)}, f32[1024,64]{1,0:T(8,128)}, f32[1024,64]{1,0:T(8,128)}) fusion(f32[64]{0:T(128)S(1)} %negate_power_fusion, f32[1024]{0:T(1024)S(1)} %fusion.5), kind=kLoop, calls=%fused_computation.7 | loop fusion | flops 131072 | bytes 790784 | tf_op jit(solution)/shard_map/neg | solution.py:33
  168.3 1.0 copy.21.refs_6_
  169.3 0.9 dynamic_slice.7
  171.0 1.9 pad_maximum_fusion.3
  173.6 13.1 %collective-permute-start.22 = (bf16[512,512]{1,0:T(8,128)(2,1)}, bf16[512,512]{1,0:T(8,128)(2,1)S(1)}, u32[]{:S(2)}, u32[]{:S(2)}) collective-permute-start(bf16[512,512]{1,0:T(8,128)(2,1)} %copy-done.27), channel_id=1, source_target_pairs={{0,7},{1,6},{2,5},{3,4},{4,3},{5,2},{6,1},{7,0},{8,15},{9,14},{10,... | collective-permute-start | bytes 1572872 | tf_op jit(solution)/shard_map/ppermute | solution.py:268
  187.0 2.4 collective-permute-done.25.refs_2_
  189.5 0.9 collective-permute-start.20
  190.3 21.5 %collective-permute-done.24.refs_1_ = bf16[512,512]{1,0:T(8,128)(2,1)} collective-permute-done((bf16[512,512]{1,0:T(8,128)(2,1)}, bf16[512,512]{1,0:T(8,128)(2,1)}, u32[]{:S(2)}, u32[]{:S(2)}) %collective-permute-start.24) | collective-permute-done | bytes 524320 | tf_op jit(solution)/shard_map/ppermute | solution.py:268
  211.9 1.0 copy-done.18
  212.9 1.0 copy-done.20
  214.0 1.0 copy-done.22
  215.0 8.5 %shard_map.96 = (f32[8192,512]{1,0:T(8,128)}, f32[1024,512]{1,0:T(8,128)}) custom-call(s32[1]{0:T(128)} %bitcast.me_ref, bf16[32,512]{1,0:T(8,128)(2,1)S(1)} %constant_dynamic-slice_fusion.b_ref, f32[1,512]{1,0:T(1,128)S(1)} %bitcast.59, f32[1,512]{1,0:T(1,128)S(1)} %fusion.6.total_ref, bf16[512,512]{1,0:T(8,128)(2,1)S(1)} %copy-done.12, ...), custom_call_target="tpu_custom_call" | custom-call | flops 3221225472 | bytes 15728640 | tf_op jit(solution)/shard_map/pallas_call | solution.py:229
  223.6 9.5 %shard_map.97 = (f32[8192,512]{1,0:T(8,128)}, f32[1024,512]{1,0:T(8,128)}) custom-call(s32[1]{0:T(128)} %bitcast.me_ref, bf16[32,512]{1,0:T(8,128)(2,1)S(1)} %constant_dynamic-slice_fusion.b_ref, f32[1,512]{1,0:T(1,128)S(1)} %bitcast.60, f32[1,512]{1,0:T(1,128)S(1)} %fusion.6.total_ref, ...), custom_call_target="tpu_custom_call", output_to_operand_aliasing={{0}: (14, {})} | custom-call | flops 2684354560 | bytes 13107200 | tf_op jit(solution)/shard_map/pallas_call | solution.py:229
  233.2 5.5 %shard_map.98 = (f32[8192,512]{1,0:T(8,128)}, f32[1024,512]{1,0:T(8,128)S(1)}) custom-call(s32[1]{0:T(128)} %bitcast.me_ref, bf16[32,512]{1,0:T(8,128)(2,1)S(1)} %constant_dynamic-slice_fusion.b_ref, f32[1,512]{1,0:T(1,128)S(1)} %bitcast.61, f32[1,512]{1,0:T(1,128)S(1)} %fusion.6.total_ref, ...), custom_call_target="tpu_custom_call", output_to_operand_aliasing={{0}: (11, {})} | custom-call | flops 1610612736 | bytes 7864320 | tf_op jit(solution)/shard_map/pallas_call | solution.py:229
  238.7 1.3 copy-done.7
  240.0 4.9 %collective-permute-done.20.refs_1_ = bf16[512,512]{1,0:T(8,128)(2,1)S(1)} collective-permute-done((bf16[512,512]{1,0:T(8,128)(2,1)}, bf16[512,512]{1,0:T(8,128)(2,1)S(1)}, u32[]{:S(2)}, u32[]{:S(2)}) %collective-permute-start.20) | collective-permute-done | bytes 524320 | tf_op jit(solution)/shard_map/ppermute | solution.py:268
  244.9 20.6 %collective-permute-done.19.refs_0_ = bf16[512,512]{1,0:T(8,128)(2,1)S(1)} collective-permute-done((bf16[512,512]{1,0:T(8,128)(2,1)}, bf16[512,512]{1,0:T(8,128)(2,1)S(1)}, u32[]{:S(2)}, u32[]{:S(2)}) %collective-permute-start.19) | collective-permute-done | bytes 524320 | tf_op jit(solution)/shard_map/ppermute | solution.py:268
  265.6 13.4 %shard_map.99 = (f32[8192,512]{1,0:T(8,128)}, bf16[1024,512]{1,0:T(8,128)(2,1)}) custom-call(s32[1]{0:T(128)} %bitcast.me_ref, bf16[32,512]{1,0:T(8,128)(2,1)S(1)} %constant_dynamic-slice_fusion.b_ref, f32[1,512]{1,0:T(1,128)S(1)} %bitcast.62, f32[1,512]{1,0:T(1,128)S(1)} %fusion.6.total_ref, ...), custom_call_target="tpu_custom_call", output_to_operand_aliasing={{0}: (14, {})} | custom-call | flops 1073741824 | bytes 5242880 | tf_op jit(solution)/shard_map/pallas_call | solution.py:229
  (116 shorter events, 6.9 us)
Async XLA Ops:
  0.6 9.5 %copy-start.43 = (bf16[512,32]{0,1:T(8,128)(2,1)S(1)}, bf16[512,32]{0,1:T(8,128)(2,1)}, u32[]{:S(2)}) copy-start(bf16[512,32]{0,1:T(8,128)(2,1)} %param.10) | copy-start | bytes 98308
  3.0 18.4 %copy-start.3 = (bf16[1056,512]{1,0:T(8,128)(2,1)}, bf16[1056,512]{1,0:T(8,128)(2,1)S(1)}, u32[]{:S(2)}) copy-start(bf16[1056,512]{1,0:T(8,128)(2,1)S(1)} %get-tuple-element.89.refs_6_) | copy-start | bytes 3244036
  3.0 52.3 %collective-permute-start.3 = (bf16[1056,512]{1,0:T(8,128)(2,1)S(1)}, bf16[1056,512]{1,0:T(8,128)(2,1)}, u32[]{:S(2)}, u32[]{:S(2)}) collective-permute-start(bf16[1056,512]{1,0:T(8,128)(2,1)S(1)} %get-tuple-element.89.refs_6_), channel_id=1, source_target_pairs={{0,8},{1,9},{2,10},{3,11},{4,12},{5,13},{6,14},{7,15},{8,0},{9,1},... | collective-permute-start | bytes 3244040 | tf_op jit(solution)/shard_map/ppermute | solution.py:268
  7.1 48.2 %collective-permute-start.4 = (bf16[1056,512]{1,0:T(8,128)(2,1)S(1)}, bf16[1056,512]{1,0:T(8,128)(2,1)S(1)}, u32[]{:S(2)}, u32[]{:S(2)}) collective-permute-start(bf16[1056,512]{1,0:T(8,128)(2,1)S(1)} %get-tuple-element.89.refs_6_), channel_id=1, source_target_pairs={{0,4},{1,5},{2,6},{3,7},{4,0},{5,1},{6,2},{7,3},{8,12},{9,13},{10,... | collective-permute-start | bytes 3244040 | tf_op jit(solution)/shard_map/ppermute | solution.py:268
  8.6 46.7 %collective-permute-start.5 = (bf16[1056,512]{1,0:T(8,128)(2,1)S(1)}, bf16[1056,512]{1,0:T(8,128)(2,1)}, u32[]{:S(2)}, u32[]{:S(2)}) collective-permute-start(bf16[1056,512]{1,0:T(8,128)(2,1)S(1)} %get-tuple-element.89.refs_6_), channel_id=1, source_target_pairs={{0,2},{1,3},{2,0},{3,1},{4,6},{5,7},{6,4},{7,5},{8,10},{9,11},{10,... | collective-permute-start | bytes 3244040 | tf_op jit(solution)/shard_map/ppermute | solution.py:268
  10.3 3.4 %copy-start = (bf16[512,8192]{1,0:T(8,128)(2,1)S(1)}, bf16[512,8192]{1,0:T(8,128)(2,1)}, u32[]{:S(2)}) copy-start(bf16[512,8192]{1,0:T(8,128)(2,1)} %w_ref.1) | copy-start | bytes 25165828
  13.7 1.0 copy-start.8
  21.4 0.8 copy-start.11
  23.0 0.8 copy-start.25
  24.7 0.8 copy-start.27
  25.5 0.8 copy-start.28
  27.1 0.8 copy-start.30
  29.5 0.8 copy-start.33
  30.3 0.8 copy-start.35
  33.4 0.8 copy-start.41
  34.3 1.2 collective-permute-start
  34.4 20.1 %collective-permute-start.6 = (bf16[512,512]{1,0:T(8,128)(2,1)}, bf16[512,512]{1,0:T(8,128)(2,1)S(1)}, u32[]{:S(2)}, u32[]{:S(2)}) collective-permute-start(bf16[512,512]{1,0:T(8,128)(2,1)} %copy-done.41), channel_id=1, source_target_pairs={{0,2},{1,3},{2,0},{3,1},{4,6},{5,7},{6,4},{7,5},{8,10},{9,11},{10,... | collective-permute-start | bytes 1572872 | tf_op jit(solution)/shard_map/ppermute | solution.py:268
  35.6 13.5 %collective-permute-start.1 = (f32[4,512]{1,0:T(4,128)S(1)}, f32[4,512]{1,0:T(4,128)S(1)}, u32[]{:S(2)}, u32[]{:S(2)}) collective-permute-start(f32[4,512]{1,0:T(4,128)S(1)} %bitcast.66), channel_id=1, source_target_pairs={{0,2},{1,3},{2,0},{3,1},{4,6},{5,7},{6,4},{7,5},{8,10},{9,11},{10,... | collective-permute-start | bytes 24584 | tf_op jit(solution)/shard_map/ppermute | solution.py:268
  49.2 5.3 %collective-permute-start.2 = (f32[2,512]{1,0:T(2,128)S(1)}, f32[2,512]{1,0:T(2,128)S(1)}, u32[]{:S(2)}, u32[]{:S(2)}) collective-permute-start(f32[2,512]{1,0:T(2,128)S(1)} %bitcast.67), channel_id=1, source_target_pairs={{0,4},{1,5},{2,6},{3,7},{4,0},{5,1},{6,2},{7,3},{8,12},{9,13},{10,... | collective-permute-start | bytes 12296 | tf_op jit(solution)/shard_map/ppermute | solution.py:268
  54.5 0.8 copy-start.13
  55.3 48.7 %collective-permute-start.8 = (bf16[1056,512]{1,0:T(8,128)(2,1)S(1)}, bf16[1056,512]{1,0:T(8,128)(2,1)S(1)}, u32[]{:S(2)}, u32[]{:S(2)}) collective-permute-start(bf16[1056,512]{1,0:T(8,128)(2,1)S(1)} %collective-permute-done.4.refs_7_), channel_id=1, source_target_pairs={{0,2},{1,3},{2,0},{3,1},{4,6},{5,7},{6,4},{7,5},{8,10},{9,11},{10,... | collective-permute-start | bytes 3244040 | tf_op jit(solution)/shard_map/ppermute | solution.py:268
  56.9 48.1 %collective-permute-start.7 = (bf16[1056,512]{1,0:T(8,128)(2,1)}, bf16[1056,512]{1,0:T(8,128)(2,1)S(1)}, u32[]{:S(2)}, u32[]{:S(2)}) collective-permute-start(bf16[1056,512]{1,0:T(8,128)(2,1)} %collective-permute-done.3.refs_8_), channel_id=1, source_target_pairs={{0,4},{1,5},{2,6},{3,7},{4,0},{5,1},{6,2},{7,3},{8,12},{9,13},{10,... | collective-permute-start | bytes 3244040 | tf_op jit(solution)/shard_map/ppermute | solution.py:268
  58.4 46.7 %collective-permute-start.9 = (bf16[1056,512]{1,0:T(8,128)(2,1)}, bf16[1056,512]{1,0:T(8,128)(2,1)S(1)}, u32[]{:S(2)}, u32[]{:S(2)}) collective-permute-start(bf16[1056,512]{1,0:T(8,128)(2,1)} %collective-permute-done.3.refs_8_), channel_id=1, source_target_pairs={{0,2},{1,3},{2,0},{3,1},{4,6},{5,7},{6,4},{7,5},{8,10},{9,11},{10,... | collective-permute-start | bytes 3244040 | tf_op jit(solution)/shard_map/ppermute | solution.py:268
  58.9 37.1 %collective-permute-start.11 = (bf16[512,512]{1,0:T(8,128)(2,1)}, bf16[512,512]{1,0:T(8,128)(2,1)S(1)}, u32[]{:S(2)}, u32[]{:S(2)}) collective-permute-start(bf16[512,512]{1,0:T(8,128)(2,1)} %copy-done.40), channel_id=1, source_target_pairs={{0,12},{1,13},{2,14},{3,15},{4,8},{5,9},{6,10},{7,11},{8,4},{9,5},... | collective-permute-start | bytes 1572872 | tf_op jit(solution)/shard_map/ppermute | solution.py:268
  60.2 42.9 %collective-permute-start.10 = (bf16[512,512]{1,0:T(8,128)(2,1)}, bf16[512,512]{1,0:T(8,128)(2,1)S(1)}, u32[]{:S(2)}, u32[]{:S(2)}) collective-permute-start(bf16[512,512]{1,0:T(8,128)(2,1)} %copy-done.39), channel_id=1, source_target_pairs={{0,8},{1,9},{2,10},{3,11},{4,12},{5,13},{6,14},{7,15},{8,0},{9,1},... | collective-permute-start | bytes 1572872 | tf_op jit(solution)/shard_map/ppermute | solution.py:268
  60.9 47.5 %copy-start.38 = (bf16[512,512]{1,0:T(8,128)(2,1)S(1)}, bf16[512,512]{1,0:T(8,128)(2,1)}, u32[]{:S(2)}) copy-start(bf16[512,512]{1,0:T(8,128)(2,1)} %copy-done.37) | copy-start | bytes 1572868
  60.9 47.5 %copy-start.36 = (bf16[512,512]{1,0:T(8,128)(2,1)S(1)}, bf16[512,512]{1,0:T(8,128)(2,1)}, u32[]{:S(2)}) copy-start(bf16[512,512]{1,0:T(8,128)(2,1)} %copy-done.35) | copy-start | bytes 1572868
  60.9 49.7 %copy-start.34 = (bf16[512,512]{1,0:T(8,128)(2,1)S(1)}, bf16[512,512]{1,0:T(8,128)(2,1)}, u32[]{:S(2)}) copy-start(bf16[512,512]{1,0:T(8,128)(2,1)} %copy-done.33) | copy-start | bytes 1572868
  96.0 0.8 copy-start.15
  103.2 0.8 copy-start.17
  105.1 30.1 %copy-start.42 = (bf16[1056,512]{1,0:T(8,128)(2,1)}, bf16[1056,512]{1,0:T(8,128)(2,1)S(1)}, u32[]{:S(2)}) copy-start(bf16[1056,512]{1,0:T(8,128)(2,1)S(1)} %collective-permute-done.7.refs_9_) | copy-start | bytes 3244036
  105.1 53.4 %collective-permute-start.13 = (bf16[4,1056,512]{2,1,0:T(8,128)(2,1)S(1)}, bf16[4,1056,512]{2,1,0:T(8,128)(2,1)}, u32[]{:S(2)}, u32[]{:S(2)}) collective-permute-start(bf16[4,1056,512]{2,1,0:T(8,128)(2,1)S(1)} %pad_maximum_fusion), channel_id=1, source_target_pairs={{0,1},{1,0},{2,3},{3,2},{4,5},{5,4},{6,7},{7,6},{8,9},{9,8},{10,11... | collective-permute-start | bytes 12976136 | tf_op jit(solution)/shard_map/ppermute | solution.py:268
  105.1 27.7 %collective-permute-start.12 = (bf16[1056,512]{1,0:T(8,128)(2,1)S(1)}, bf16[1056,512]{1,0:T(8,128)(2,1)S(1)}, u32[]{:S(2)}, u32[]{:S(2)}) collective-permute-start(bf16[1056,512]{1,0:T(8,128)(2,1)S(1)} %collective-permute-done.7.refs_9_), channel_id=1, source_target_pairs={{0,2},{1,3},{2,0},{3,1},{4,6},{5,7},{6,4},{7,5},{8,10},{9,11},{10,... | collective-permute-start | bytes 3244040 | tf_op jit(solution)/shard_map/ppermute | solution.py:268
  108.3 26.9 %collective-permute-start.16 = (bf16[512,512]{1,0:T(8,128)(2,1)S(1)}, bf16[512,512]{1,0:T(8,128)(2,1)S(1)}, u32[]{:S(2)}, u32[]{:S(2)}) collective-permute-start(bf16[512,512]{1,0:T(8,128)(2,1)S(1)} %copy-done.38), channel_id=1, source_target_pairs={{0,4},{1,5},{2,6},{3,7},{4,0},{5,1},{6,2},{7,3},{8,12},{9,13},{10,... | collective-permute-start | bytes 1572872 | tf_op jit(solution)/shard_map/ppermute | solution.py:268
  108.3 27.7 %collective-permute-start.15 = (bf16[512,512]{1,0:T(8,128)(2,1)S(1)}, bf16[512,512]{1,0:T(8,128)(2,1)S(1)}, u32[]{:S(2)}, u32[]{:S(2)}) collective-permute-start(bf16[512,512]{1,0:T(8,128)(2,1)S(1)} %copy-done.36), channel_id=1, source_target_pairs={{0,13},{1,12},{2,15},{3,14},{4,9},{5,8},{6,11},{7,10},{8,5},{9,4},... | collective-permute-start | bytes 1572872 | tf_op jit(solution)/shard_map/ppermute | solution.py:268
  110.6 47.1 %collective-permute-start.14 = (bf16[512,512]{1,0:T(8,128)(2,1)S(1)}, bf16[512,512]{1,0:T(8,128)(2,1)S(1)}, u32[]{:S(2)}, u32[]{:S(2)}) collective-permute-start(bf16[512,512]{1,0:T(8,128)(2,1)S(1)} %copy-done.34), channel_id=1, source_target_pairs={{0,9},{1,8},{2,11},{3,10},{4,13},{5,12},{6,15},{7,14},{8,1},{9,0},... | collective-permute-start | bytes 1572872 | tf_op jit(solution)/shard_map/ppermute | solution.py:268
  132.8 2.4 copy-start.1
  132.8 25.9 %copy-start.23 = (s32[1024]{0:T(1024)S(1)}, s32[1024]{0:T(1024)}, u32[]{:S(2)}) copy-start(s32[1024]{0:T(1024)} %param.13) | copy-start | bytes 12292
  135.2 0.8 copy-start.19
  136.0 0.8 copy-start.9
  157.7 0.9 copy-start.21
  158.5 14.4 %collective-permute-start.18 = (bf16[4,1056,512]{2,1,0:T(8,128)(2,1)}, bf16[4,1056,512]{2,1,0:T(8,128)(2,1)}, u32[]{:S(2)}, u32[]{:S(2)}) collective-permute-start(bf16[4,1056,512]{2,1,0:T(8,128)(2,1)} %pad_maximum_fusion.1), channel_id=1, source_target_pairs={{0,1},{1,0},{2,3},{3,2},{4,5},{5,4},{6,7},{7,6},{8,9},{9,8},{10,11... | collective-permute-start | bytes 12976136 | tf_op jit(solution)/shard_map/ppermute | solution.py:268
  159.4 5.7 %collective-permute-start.17 = (f32[1,512]{1,0:T(1,128)S(1)}, f32[1,512]{1,0:T(1,128)S(1)}, u32[]{:S(2)}, u32[]{:S(2)}) collective-permute-start(f32[1,512]{1,0:T(1,128)S(1)} %slice_bitcast_fusion), channel_id=1, source_target_pairs={{0,8},{1,9},{2,10},{3,11},{4,12},{5,13},{6,14},{7,15},{8,0},{9,1},... | collective-permute-start | bytes 6152 | tf_op jit(solution)/shard_map/ppermute | solution.py:268
  159.5 14.2 %collective-permute-start.27 = (bf16[512,512]{1,0:T(8,128)(2,1)}, bf16[512,512]{1,0:T(8,128)(2,1)}, u32[]{:S(2)}, u32[]{:S(2)}) collective-permute-start(bf16[512,512]{1,0:T(8,128)(2,1)} %copy-done.32), channel_id=1, source_target_pairs={{0,3},{1,2},{2,1},{3,0},{4,7},{5,6},{6,5},{7,4},{8,11},{9,10},{10,... | collective-permute-start | bytes 1572872 | tf_op jit(solution)/shard_map/ppermute | solution.py:268
  159.6 27.2 %collective-permute-start.26 = (bf16[512,512]{1,0:T(8,128)(2,1)}, bf16[512,512]{1,0:T(8,128)(2,1)}, u32[]{:S(2)}, u32[]{:S(2)}) collective-permute-start(bf16[512,512]{1,0:T(8,128)(2,1)} %copy-done.31), channel_id=1, source_target_pairs={{0,5},{1,4},{2,7},{3,6},{4,1},{5,0},{6,3},{7,2},{8,13},{9,12},{10,... | collective-permute-start | bytes 1572872 | tf_op jit(solution)/shard_map/ppermute | solution.py:268
  162.7 26.7 %collective-permute-start.25 = (bf16[512,512]{1,0:T(8,128)(2,1)}, bf16[512,512]{1,0:T(8,128)(2,1)}, u32[]{:S(2)}, u32[]{:S(2)}) collective-permute-start(bf16[512,512]{1,0:T(8,128)(2,1)} %copy-done.30), channel_id=1, source_target_pairs={{0,14},{1,15},{2,12},{3,13},{4,10},{5,11},{6,8},{7,9},{8,6},{9,7},... | collective-permute-start | bytes 1572872 | tf_op jit(solution)/shard_map/ppermute | solution.py:268
  165.1 46.8 %collective-permute-start.24 = (bf16[512,512]{1,0:T(8,128)(2,1)}, bf16[512,512]{1,0:T(8,128)(2,1)}, u32[]{:S(2)}, u32[]{:S(2)}) collective-permute-start(bf16[512,512]{1,0:T(8,128)(2,1)} %copy-done.29), channel_id=1, source_target_pairs={{0,10},{1,11},{2,8},{3,9},{4,14},{5,15},{6,12},{7,13},{8,2},{9,3},... | collective-permute-start | bytes 1572872 | tf_op jit(solution)/shard_map/ppermute | solution.py:268
  169.3 42.5 %copy-start.4 = (bf16[1056,512]{1,0:T(8,128)(2,1)S(1)}, bf16[1056,512]{1,0:T(8,128)(2,1)}, u32[]{:S(2)}) copy-start(bf16[1056,512]{1,0:T(8,128)(2,1)} %copy-done.3) | copy-start | bytes 3244036
  169.3 42.5 %copy-start.12 = (bf16[512,512]{1,0:T(8,128)(2,1)S(1)}, bf16[512,512]{1,0:T(8,128)(2,1)}, u32[]{:S(2)}) copy-start(bf16[512,512]{1,0:T(8,128)(2,1)} %copy-done.11) | copy-start | bytes 1572868
  169.3 42.5 %copy-start.14 = (bf16[512,512]{1,0:T(8,128)(2,1)S(1)}, bf16[512,512]{1,0:T(8,128)(2,1)}, u32[]{:S(2)}) copy-start(bf16[512,512]{1,0:T(8,128)(2,1)} %copy-done.13) | copy-start | bytes 1572868
  169.3 42.5 %copy-start.16 = (bf16[512,512]{1,0:T(8,128)(2,1)S(1)}, bf16[512,512]{1,0:T(8,128)(2,1)}, u32[]{:S(2)}) copy-start(bf16[512,512]{1,0:T(8,128)(2,1)} %copy-done.15) | copy-start | bytes 1572868
  172.9 60.2 %collective-permute-start.23 = (bf16[512,512]{1,0:T(8,128)(2,1)}, bf16[512,512]{1,0:T(8,128)(2,1)S(1)}, u32[]{:S(2)}, u32[]{:S(2)}) collective-permute-start(bf16[512,512]{1,0:T(8,128)(2,1)} %copy-done.28), channel_id=1, source_target_pairs={{0,1},{1,0},{2,3},{3,2},{4,5},{5,4},{6,7},{7,6},{8,9},{9,8},{10,11... | collective-permute-start | bytes 1572872 | tf_op jit(solution)/shard_map/ppermute | solution.py:268
  173.6 59.5 %collective-permute-start.22 = (bf16[512,512]{1,0:T(8,128)(2,1)}, bf16[512,512]{1,0:T(8,128)(2,1)S(1)}, u32[]{:S(2)}, u32[]{:S(2)}) collective-permute-start(bf16[512,512]{1,0:T(8,128)(2,1)} %copy-done.27), channel_id=1, source_target_pairs={{0,7},{1,6},{2,5},{3,4},{4,3},{5,2},{6,1},{7,0},{8,15},{9,14},{10,... | collective-permute-start | bytes 1572872 | tf_op jit(solution)/shard_map/ppermute | solution.py:268
  186.8 46.3 %collective-permute-start.21 = (bf16[512,512]{1,0:T(8,128)(2,1)}, bf16[512,512]{1,0:T(8,128)(2,1)S(1)}, u32[]{:S(2)}, u32[]{:S(2)}) collective-permute-start(bf16[512,512]{1,0:T(8,128)(2,1)} %copy-done.26), channel_id=1, source_target_pairs={{0,6},{1,7},{2,4},{3,5},{4,2},{5,3},{6,0},{7,1},{8,14},{9,15},{10,... | collective-permute-start | bytes 1572872 | tf_op jit(solution)/shard_map/ppermute | solution.py:268
  189.5 55.5 %collective-permute-start.20 = (bf16[512,512]{1,0:T(8,128)(2,1)}, bf16[512,512]{1,0:T(8,128)(2,1)S(1)}, u32[]{:S(2)}, u32[]{:S(2)}) collective-permute-start(bf16[512,512]{1,0:T(8,128)(2,1)} %copy-done.25), channel_id=1, source_target_pairs={{0,15},{1,14},{2,13},{3,12},{4,11},{5,10},{6,9},{7,8},{8,7},{9,6},... | collective-permute-start | bytes 1572872 | tf_op jit(solution)/shard_map/ppermute | solution.py:268
  211.9 53.7 %collective-permute-start.19 = (bf16[512,512]{1,0:T(8,128)(2,1)}, bf16[512,512]{1,0:T(8,128)(2,1)S(1)}, u32[]{:S(2)}, u32[]{:S(2)}) collective-permute-start(bf16[512,512]{1,0:T(8,128)(2,1)} %copy-done.24), channel_id=1, source_target_pairs={{0,11},{1,10},{2,9},{3,8},{4,15},{5,14},{6,13},{7,12},{8,3},{9,2},... | collective-permute-start | bytes 1572872 | tf_op jit(solution)/shard_map/ppermute | solution.py:268
  211.9 1.0 copy-start.18
  212.9 1.0 copy-start.20
  214.0 1.0 copy-start.22
  215.0 8.5 %copy-start.2 = (bf16[1056,512]{1,0:T(8,128)(2,1)S(1)}, bf16[1056,512]{1,0:T(8,128)(2,1)}, u32[]{:S(2)}) copy-start(bf16[1056,512]{1,0:T(8,128)(2,1)} %copy-done.1) | copy-start | bytes 3244036
  215.0 8.5 %copy-start.10 = (bf16[512,512]{1,0:T(8,128)(2,1)S(1)}, bf16[512,512]{1,0:T(8,128)(2,1)}, u32[]{:S(2)}) copy-start(bf16[512,512]{1,0:T(8,128)(2,1)} %copy-done.9) | copy-start | bytes 1572868
  233.1 32.4 %copy-start.5 = (s32[1024,1]{1,0:T(8,128)S(1)}, s32[1024,1]{1,0:T(8,128)}, u32[]{:S(2)}) copy-start(s32[1024,1]{1,0:T(8,128)} %copy.21.refs_6_) | copy-start | bytes 12292
  233.1 32.4 %copy-start.6 = (bf16[1024,1024]{1,0:T(8,128)(2,1)S(1)}, bf16[1024,1024]{1,0:T(8,128)(2,1)}, u32[]{:S(2)}) copy-start(bf16[1024,1024]{1,0:T(8,128)(2,1)} %refs_7_.1) | copy-start | bytes 6291460
  238.7 1.3 copy-start.7
  (8 other events, 6.3 us)

commit v2 on v1

--- a/solution.py
+++ b/solution.py
@@ -1,4 +1,5 @@
 import functools
+import math
 
 import jax
 import jax.numpy as jnp
@@ -11,7 +12,7 @@
 KVH = 8
 GROUP = 8
 DOC_MAX = 512
-Q_BLOCK = 256
+Q_BLOCK = 128
 
 
 def doc_positions(token_document_index):
@@ -94,7 +95,7 @@
     (merged_ref, q_out), refs = refs[:2], refs[2:]
     (w_buf, x_buf, a_buf, u_buf, w_sem, x_sem, a_sem, m_sem), refs = refs[:8], refs[8:]
     if last:
-        q_buf, k_buf, v_buf, k_sem, q_sem, o_sem = refs
+        q_buf, k_buf, v_buf, k_sem = refs
     else:
         q_buf = q_out
     tokens = x_buf.shape[1]
@@ -132,9 +133,6 @@
         ]
         for copy in kv_copies:
             copy.start()
-        if not first:
-            q_copy = pltpu.make_async_copy(q_in, q_buf, q_sem)
-            q_copy.start()
 
     scale = mag_ref[...] / jnp.sqrt(total_ref[...] + 1e-06)
     for k in range(count):
@@ -148,14 +146,12 @@
         out_copy(k).start()
         x_copy(k).wait()
         product = jnp.dot(x_buf[k], merged.astype(jnp.bfloat16), preferred_element_type=jnp.float32)
-        if k == 0 and first:
+        if k > 0:
+            q_buf[...] += product
+        elif first:
             q_buf[...] = product
-        elif k == 0 and not last:
+        else:
             q_buf[...] = q_in[...] + product
-        else:
-            if k == 0:
-                q_copy.wait()
-            q_buf[...] += product
 
     if last:
         for copy in kv_copies:
@@ -167,6 +163,7 @@
 
 def attend(q_ref, cos_ref, sin_ref, row_ref, col_ref, k_ref, v_ref, att_ref, local):
     tokens = q_ref.shape[0]
+    turns = jnp.float32(HD**-0.5 * math.log2(math.e))
     for t in range(0, tokens, Q_BLOCK):
         low, high = max(0, t - DOC_MAX), t + Q_BLOCK
         shape = (Q_BLOCK, high - low)
@@ -175,24 +172,28 @@
             row_ref[:, pl.ds(low, high - low)] == col_ref[pl.ds(t, Q_BLOCK), :]
         )
         cosine, sine = cos_ref[pl.ds(t, Q_BLOCK), :], sin_ref[pl.ds(t, Q_BLOCK), :]
+        rotated = []
         for h in range(local):
-            lanes = pl.ds(h * HD, HD)
-            query = q_ref[pl.ds(t, Q_BLOCK), lanes]
+            query = q_ref[pl.ds(t, Q_BLOCK), pl.ds(h * HD, HD)]
             turned = pltpu.roll(query, HD // 2, 1)
-            rotated = (query * cosine + turned * sine).astype(jnp.bfloat16)
-            scores = lax.dot_general(
-                rotated,
-                k_ref[pl.ds(low, high - low), :],
-                (((1,), (1,)), ((), ())),
-                preferred_element_type=jnp.float32,
-            ) * jnp.float32(HD**-0.5)
-            scores = jnp.where(allowed, scores, -jnp.inf)
-            top = jnp.max(scores, axis=1, keepdims=True)
-            weights = jnp.exp(scores - top)
-            probs = (weights / jnp.sum(weights, axis=1, keepdims=True)).astype(jnp.bfloat16)
-            att_ref[pl.ds(t, Q_BLOCK), lanes] = jnp.dot(
-                probs, v_ref[pl.ds(low, high - low), :], preferred_element_type=jnp.float32
-            ).astype(jnp.bfloat16)
+            rotated.append((query * cosine + turned * sine).astype(jnp.bfloat16))
+        scores = lax.dot_general(
+            jnp.concatenate(rotated, axis=0),
+            k_ref[pl.ds(low, high - low), :],
+            (((1,), (1,)), ((), ())),
+            preferred_element_type=jnp.float32,
+        ).reshape(local, *shape)
+        scores = jnp.where(allowed[None], scores, -jnp.inf)
+        top = jnp.max(scores, axis=2, keepdims=True)
+        weights = jnp.exp2((scores - top) * turns)
+        share = 1.0 / jnp.sum(weights, axis=2, keepdims=True)
+        out = jnp.dot(
+            (weights * share).astype(jnp.bfloat16).reshape(local * Q_BLOCK, high - low),
+            v_ref[pl.ds(low, high - low), :],
+            preferred_element_type=jnp.float32,
+        ).astype(jnp.bfloat16)
+        for h in range(local):
+            att_ref[pl.ds(t, Q_BLOCK), pl.ds(h * HD, HD)] = out[h * Q_BLOCK : (h + 1) * Q_BLOCK]
 
 
 def merge(me, b, mag, total, slots, w_list, w_at, x_list, x_at, sizes, xor, previous=None, attention=None):
@@ -217,14 +218,12 @@
             pltpu.VMEM((tokens, HD), jnp.bfloat16),
             pltpu.VMEM((tokens, HD), jnp.bfloat16),
             pltpu.SemaphoreType.DMA((2,)),
-            pltpu.SemaphoreType.DMA,
-            pltpu.SemaphoreType.DMA,
         ]
     aliases = {}
     if not first:
         merged, query = previous
         operands += [query, merged]
-        in_specs += [hbm if last else vmem, hbm]
+        in_specs += [vmem, hbm]
         aliases = {len(operands) - 1: 0}
     return pl.pallas_call(
         functools.partial(merge_kernel, plan),
@@ -254,13 +253,13 @@
 ROUNDS = (
     ("z2", "z1", "y0", "s1", "w2", "s2", "s4"),
     ("z3", "y1", "y2", "w8", "w12"),
-    ("y3", "cA", "w9", "w13", "w4"),
-    ("cD", "w10", "w14", "w5", "w3", "s8"),
-    ("w11", "w15", "w6", "w7", "w1"),
+    ("y3", "cA", "w4", "w9", "w13"),
+    ("cD", "s8", "w3", "w6", "w10", "w14"),
+    ("w1", "w5", "w7", "w11", "w15"),
 )
 LINES = {"z1": ("x", 4), "z2": ("x", 8), "z3": ("z2", 4), "y0": ("x", 2), "y1": ("z1", 2), "y2": ("z2", 2), "y3": ("z3", 2)}
 STACKS = {"cA": ("x", "z1", "z2", "y0"), "cD": ("z3", "y1", "y2", "y3")}
-GROUPS = ((0, 8, 12, 4, 9, 2), (13, 10, 14, 5, 3), (6, 7, 1), (11, 15))
+GROUPS = ((0, 8, 12, 4, 9, 2), (13, 10, 14, 6, 3), (5, 7, 1, 15), (11,))
 
 
 def exchange(x, blocks, sums):
@@ -279,7 +278,7 @@
         return (partial[:, 1] if name[0] == "s" else blocks[d]), d
 
     def heavy(name):
-        return name[0] == "w"
+        return name[0] in "ws"
 
     for k, names in enumerate(ROUNDS):
         new = {}

time: 280 us -> 273 us (0.975)
  waiting for transfers between devices: 150 us -> 124 us
  starting transfers between devices: 41.4 us -> 61.6 us
    ppermute x28, waiting for transfers between devices: 150 us -> 124 us  [swap(): return lax.ppermute(array, 'tensor', [(i, i ^ d) for i in range(16)])]
    ppermute x28, starting transfers between devices: 41.4 us -> 61.6 us  [swap(): return lax.ppermute(array, 'tensor', [(i, i ^ d) for i in range(16)])]
  transfers between devices with their start and end apart: 28 -> 28, of which waited for: 13 -> 11; matrix products, arithmetic and copies ran while one was open for 5% -> 5% of each run, Pallas kernels for 11% -> 12%
where the time goes in v2:
time: 273 us; the launch traced here: 272 us
  waiting for transfers between devices  124 us (45%)
  starting transfers between devices  61.6 us (23%)
  Pallas kernels  42 us (15%)
  local copies, waits for them, and re-layouts  31 us (11%)
  other arithmetic  12.6 us (5%)
    ppermute x28, waiting for transfers between devices, swap(): return lax.ppermute(array, 'tensor', [(i, i ^ d) for i in range(16)])  124 us
    ppermute x28, starting transfers between devices, swap(): return lax.ppermute(array, 'tensor', [(i, i ^ d) for i in range(16)])  61.6 us
    pallas_call x4, Pallas kernels, merge(): pl.pallas_call(functools.partial(merge_kernel, plan), out_shape=[jax.Shap...  35.3 us
    unnamed x92, local copies, waits for them, and re-layouts  28 us
    another operation x3, other arithmetic, payload(): return (jnp.stack([got[k] for k in STACKS[name]]), 1)  6.96 us
    pallas_call x1, Pallas kernels, cut(): pl.pallas_call(cut_kernel, out_shape=[jax.ShapeDtypeStruct((rows, width),...  6.71 us
  transfers between devices with their start and end apart: 28, of which 11 were waited for; matrix products, arithmetic and copies ran while one was open for 5% of the time, Pallas kernels for 12%

profile of v2, /device:TPU:0, one launch (start us, length us, event | category | flops | bytes accessed | tf_op | source)
XLA Modules:
  0.0 272.3 jit_solution(5847999480462317266)
XLA Ops:
  0.6 2.4 fusion.7
  3.0 4.0 %collective-permute-start.3 = (bf16[1056,512]{1,0:T(8,128)(2,1)S(1)}, bf16[1056,512]{1,0:T(8,128)(2,1)}, u32[]{:S(2)}, u32[]{:S(2)}) collective-permute-start(bf16[1056,512]{1,0:T(8,128)(2,1)S(1)} %get-tuple-element.89.refs_6_), channel_id=1, source_target_pairs={{0,8},{1,9},{2,10},{3,11},{4,12},{5,13},{6,14},{7,15},{8,0},{9,1},... | collective-permute-start | bytes 3244040 | tf_op jit(solution)/shard_map/ppermute | solution.py:267
  7.1 1.6 collective-permute-start.4
  8.6 1.5 collective-permute-start.5
  10.3 3.4 %copy-done = bf16[512,8192]{1,0:T(8,128)(2,1)S(1)} copy-done((bf16[512,8192]{1,0:T(8,128)(2,1)S(1)}, bf16[512,8192]{1,0:T(8,128)(2,1)}, u32[]{:S(2)}) %copy-start) | copy-done | bytes 8388632
  13.7 1.0 copy-done.8
  14.7 6.7 %shard_map.95 = (bf16[512,512]{1,0:T(8,128)(2,1)S(1)}, bf16[512,512]{1,0:T(8,128)(2,1)S(1)}, bf16[512,512]{1,0:T(8,128)(2,1)S(1)}, bf16[512,512]{1,0:T(8,128)(2,...) custom-call(s32[1]{0:T(128)} %bitcast.me_ref, ...), custom_call_target="tpu_custom_call" | custom-call | flops 16777216 | bytes 16777216 | tf_op jit(solution)/shard_map/pallas_call | solution.py:68
  21.4 0.8 copy-done.11
  22.2 0.8 copy-done.24
  23.0 0.8 copy-done.25
  23.9 0.8 copy-done.26
  24.7 0.8 copy-done.27
  25.5 0.8 copy-done.28
  26.3 0.8 copy-done.29
  27.1 0.8 copy-done.30
  29.5 0.8 copy-done.33
  31.0 0.8 copy-done.37
  31.8 0.8 copy-done.39
  32.6 0.8 copy-done.40
  33.4 0.8 copy-done.41
  35.6 1.0 collective-permute-start.1
  36.6 12.5 %collective-permute-done.1 = f32[4,512]{1,0:T(4,128)S(1)} collective-permute-done((f32[4,512]{1,0:T(4,128)S(1)}, f32[4,512]{1,0:T(4,128)S(1)}, u32[]{:S(2)}, u32[]{:S(2)}) %collective-permute-start.1) | collective-permute-done | bytes 8224 | tf_op jit(solution)/shard_map/ppermute | solution.py:267
  49.7 4.8 %collective-permute-done.2 = f32[2,512]{1,0:T(2,128)S(1)} collective-permute-done((f32[2,512]{1,0:T(2,128)S(1)}, f32[2,512]{1,0:T(2,128)S(1)}, u32[]{:S(2)}, u32[]{:S(2)}) %collective-permute-start.2) | collective-permute-done | bytes 4128 | tf_op jit(solution)/shard_map/ppermute | solution.py:267
  54.5 0.8 copy-done.13
  55.3 1.6 collective-permute-start.8
  56.9 1.4 collective-permute-start.7
  58.9 1.4 collective-permute-start.11
  60.9 2.3 pad_maximum_fusion
  63.2 32.8 %collective-permute-done.11.refs_2_ = bf16[512,512]{1,0:T(8,128)(2,1)S(1)} collective-permute-done((bf16[512,512]{1,0:T(8,128)(2,1)}, bf16[512,512]{1,0:T(8,128)(2,1)S(1)}, u32[]{:S(2)}, u32[]{:S(2)}) %collective-permute-start.11) | collective-permute-done | bytes 524320 | tf_op jit(solution)/shard_map/ppermute | solution.py:267
  95.9 0.8 copy-done.15
  96.7 6.5 %collective-permute-done.10.refs_1_ = bf16[512,512]{1,0:T(8,128)(2,1)S(1)} collective-permute-done((bf16[512,512]{1,0:T(8,128)(2,1)}, bf16[512,512]{1,0:T(8,128)(2,1)S(1)}, u32[]{:S(2)}, u32[]{:S(2)}) %collective-permute-start.10) | collective-permute-done | bytes 524320 | tf_op jit(solution)/shard_map/ppermute | solution.py:267
  103.2 1.9 collective-permute-done.7.refs_9_
  105.1 2.4 collective-permute-start.12
  107.5 2.8 %collective-permute-start.15 = (bf16[512,512]{1,0:T(8,128)(2,1)S(1)}, bf16[512,512]{1,0:T(8,128)(2,1)S(1)}, u32[]{:S(2)}, u32[]{:S(2)}) collective-permute-start(bf16[512,512]{1,0:T(8,128)(2,1)S(1)} %copy-done.36), channel_id=1, source_target_pairs={{0,4},{1,5},{2,6},{3,7},{4,0},{5,1},{6,2},{7,3},{8,12},{9,13},{10,... | collective-permute-start | bytes 1572872 | tf_op jit(solution)/shard_map/ppermute | solution.py:267
  110.3 1.0 collective-permute-start.17
  111.4 20.6 %collective-permute-done.12.refs_7_ = bf16[1056,512]{1,0:T(8,128)(2,1)S(1)} collective-permute-done((bf16[1056,512]{1,0:T(8,128)(2,1)S(1)}, bf16[1056,512]{1,0:T(8,128)(2,1)S(1)}, u32[]{:S(2)}, u32[]{:S(2)}) %collective-permute-start.12) | collective-permute-done | bytes 1081376 | tf_op jit(solution)/shard_map/ppermute | solution.py:267
  132.0 2.3 pad_maximum_fusion.1
  134.3 0.8 copy-done.19
  135.2 10.0 %collective-permute-done.15.refs_3_ = bf16[512,512]{1,0:T(8,128)(2,1)S(1)} collective-permute-done((bf16[512,512]{1,0:T(8,128)(2,1)S(1)}, bf16[512,512]{1,0:T(8,128)(2,1)S(1)}, u32[]{:S(2)}, u32[]{:S(2)}) %collective-permute-start.15) | collective-permute-done | bytes 524320 | tf_op jit(solution)/shard_map/ppermute | solution.py:267
  145.2 0.8 copy-done.21
  146.1 0.8 copy-done.9
  147.6 10.6 %collective-permute-start.14 = (f32[1,512]{1,0:T(1,128)S(1)}, f32[1,512]{1,0:T(1,128)S(1)}, u32[]{:S(2)}, u32[]{:S(2)}) collective-permute-start(f32[1,512]{1,0:T(1,128)S(1)} %slice_bitcast_fusion), channel_id=1, source_target_pairs={{0,8},{1,9},{2,10},{3,11},{4,12},{5,13},{6,14},{7,15},{8,0},{9,1},... | collective-permute-start | bytes 6152 | tf_op jit(solution)/shard_map/ppermute | solution.py:267
  158.2 0.8 collective-permute-start.27
  159.0 0.8 collective-permute-start.26
  159.8 2.0 collective-permute-start.25
  161.8 1.9 collective-permute-start.24
  163.8 3.2 %fusion = (f32[1024,64]{1,0:T(8,128)}, f32[1024,64]{1,0:T(8,128)}, f32[1024,64]{1,0:T(8,128)}) fusion(f32[64]{0:T(128)S(1)} %negate_power_fusion, f32[1024]{0:T(1024)S(1)} %fusion.5), kind=kLoop, calls=%fused_computation.7 | loop fusion | flops 131072 | bytes 790784 | tf_op jit(solution)/shard_map/neg | solution.py:34
  166.9 1.0 copy.21.refs_5_
  168.0 0.9 dynamic_slice.7
  169.7 1.9 pad_maximum_fusion.3
  171.5 1.3 collective-permute-start.23
  172.9 22.1 %collective-permute-done.27.refs_4_ = bf16[512,512]{1,0:T(8,128)(2,1)} collective-permute-done((bf16[512,512]{1,0:T(8,128)(2,1)}, bf16[512,512]{1,0:T(8,128)(2,1)}, u32[]{:S(2)}, u32[]{:S(2)}) %collective-permute-start.27) | collective-permute-done | bytes 524320 | tf_op jit(solution)/shard_map/ppermute | solution.py:267
  195.1 22.9 %collective-permute-start.20 = (bf16[512,512]{1,0:T(8,128)(2,1)}, bf16[512,512]{1,0:T(8,128)(2,1)S(1)}, u32[]{:S(2)}, u32[]{:S(2)}) collective-permute-start(bf16[512,512]{1,0:T(8,128)(2,1)} %copy-done.25), channel_id=1, source_target_pairs={{0,5},{1,4},{2,7},{3,6},{4,1},{5,0},{6,3},{7,2},{8,13},{9,12},{10,... | collective-permute-start | bytes 1572872 | tf_op jit(solution)/shard_map/ppermute | solution.py:267
  218.0 12.0 %collective-permute-done.24.refs_1_ = bf16[512,512]{1,0:T(8,128)(2,1)} collective-permute-done((bf16[512,512]{1,0:T(8,128)(2,1)}, bf16[512,512]{1,0:T(8,128)(2,1)}, u32[]{:S(2)}, u32[]{:S(2)}) %collective-permute-start.24) | collective-permute-done | bytes 524320 | tf_op jit(solution)/shard_map/ppermute | solution.py:267
  230.0 1.0 copy-done.14
  231.1 1.0 copy-done.16
  232.1 1.0 copy-done.18
  233.2 1.0 copy-done.20
  234.2 1.0 copy-done.22
  235.2 8.4 %shard_map.96 = (f32[8192,512]{1,0:T(8,128)}, f32[1024,512]{1,0:T(8,128)}) custom-call(s32[1]{0:T(128)} %bitcast.me_ref, bf16[32,512]{1,0:T(8,128)(2,1)S(1)} %constant_dynamic-slice_fusion.b_ref, f32[1,512]{1,0:T(1,128)S(1)} %bitcast.59, f32[1,512]{1,0:T(1,128)S(1)} %fusion.6.total_ref, bf16[512,512]{1,0:T(8,128)(2,1)S(1)} %copy-done.12, ...), custom_call_target="tpu_custom_call" | custom-call | flops 3221225472 | bytes 15728640 | tf_op jit(solution)/shard_map/pallas_call | solution.py:228
  243.7 9.5 %shard_map.97 = (f32[8192,512]{1,0:T(8,128)}, f32[1024,512]{1,0:T(8,128)}) custom-call(s32[1]{0:T(128)} %bitcast.me_ref, bf16[32,512]{1,0:T(8,128)(2,1)S(1)} %constant_dynamic-slice_fusion.b_ref, f32[1,512]{1,0:T(1,128)S(1)} %bitcast.60, f32[1,512]{1,0:T(1,128)S(1)} %fusion.6.total_ref, ...), custom_call_target="tpu_custom_call", output_to_operand_aliasing={{0}: (15, {})} | custom-call | flops 2684354560 | bytes 13107200 | tf_op jit(solution)/shard_map/pallas_call | solution.py:228
  253.3 7.3 %shard_map.98 = (f32[8192,512]{1,0:T(8,128)}, f32[1024,512]{1,0:T(8,128)S(1)}) custom-call(s32[1]{0:T(128)} %bitcast.me_ref, bf16[32,512]{1,0:T(8,128)(2,1)S(1)} %constant_dynamic-slice_fusion.b_ref, f32[1,512]{1,0:T(1,128)S(1)} %bitcast.61, f32[1,512]{1,0:T(1,128)S(1)} %fusion.6.total_ref, ...), custom_call_target="tpu_custom_call", output_to_operand_aliasing={{0}: (11, {})} | custom-call | flops 2147483648 | bytes 10485760 | tf_op jit(solution)/shard_map/pallas_call | solution.py:228
  260.6 1.3 copy-done.7
  262.1 10.1 %shard_map.99 = (f32[8192,512]{1,0:T(8,128)}, bf16[1024,512]{1,0:T(8,128)(2,1)}) custom-call(s32[1]{0:T(128)} %bitcast.me_ref, bf16[32,512]{1,0:T(8,128)(2,1)S(1)} %constant_dynamic-slice_fusion.b_ref, f32[1,512]{1,0:T(1,128)S(1)} %bitcast.62, f32[1,512]{1,0:T(1,128)S(1)} %fusion.6.total_ref, ...), custom_call_target="tpu_custom_call", output_to_operand_aliasing={{0}: (13, {})} | custom-call | flops 536870912 | bytes 2621440 | tf_op jit(solution)/shard_map/pallas_call | solution.py:228
  (116 shorter events, 7.5 us)
Async XLA Ops:
  0.6 9.5 %copy-start.43 = (bf16[512,32]{0,1:T(8,128)(2,1)S(1)}, bf16[512,32]{0,1:T(8,128)(2,1)}, u32[]{:S(2)}) copy-start(bf16[512,32]{0,1:T(8,128)(2,1)} %param.10) | copy-start | bytes 98308
  3.0 18.4 %copy-start.3 = (bf16[1056,512]{1,0:T(8,128)(2,1)}, bf16[1056,512]{1,0:T(8,128)(2,1)S(1)}, u32[]{:S(2)}) copy-start(bf16[1056,512]{1,0:T(8,128)(2,1)S(1)} %get-tuple-element.89.refs_6_) | copy-start | bytes 3244036
  3.0 52.3 %collective-permute-start.3 = (bf16[1056,512]{1,0:T(8,128)(2,1)S(1)}, bf16[1056,512]{1,0:T(8,128)(2,1)}, u32[]{:S(2)}, u32[]{:S(2)}) collective-permute-start(bf16[1056,512]{1,0:T(8,128)(2,1)S(1)} %get-tuple-element.89.refs_6_), channel_id=1, source_target_pairs={{0,8},{1,9},{2,10},{3,11},{4,12},{5,13},{6,14},{7,15},{8,0},{9,1},... | collective-permute-start | bytes 3244040 | tf_op jit(solution)/shard_map/ppermute | solution.py:267
  7.1 48.2 %collective-permute-start.4 = (bf16[1056,512]{1,0:T(8,128)(2,1)S(1)}, bf16[1056,512]{1,0:T(8,128)(2,1)S(1)}, u32[]{:S(2)}, u32[]{:S(2)}) collective-permute-start(bf16[1056,512]{1,0:T(8,128)(2,1)S(1)} %get-tuple-element.89.refs_6_), channel_id=1, source_target_pairs={{0,4},{1,5},{2,6},{3,7},{4,0},{5,1},{6,2},{7,3},{8,12},{9,13},{10,... | collective-permute-start | bytes 3244040 | tf_op jit(solution)/shard_map/ppermute | solution.py:267
  8.6 46.7 %collective-permute-start.5 = (bf16[1056,512]{1,0:T(8,128)(2,1)S(1)}, bf16[1056,512]{1,0:T(8,128)(2,1)}, u32[]{:S(2)}, u32[]{:S(2)}) collective-permute-start(bf16[1056,512]{1,0:T(8,128)(2,1)S(1)} %get-tuple-element.89.refs_6_), channel_id=1, source_target_pairs={{0,2},{1,3},{2,0},{3,1},{4,6},{5,7},{6,4},{7,5},{8,10},{9,11},{10,... | collective-permute-start | bytes 3244040 | tf_op jit(solution)/shard_map/ppermute | solution.py:267
  10.3 3.4 %copy-start = (bf16[512,8192]{1,0:T(8,128)(2,1)S(1)}, bf16[512,8192]{1,0:T(8,128)(2,1)}, u32[]{:S(2)}) copy-start(bf16[512,8192]{1,0:T(8,128)(2,1)} %w_ref.1) | copy-start | bytes 25165828
  13.7 1.0 copy-start.8
  21.4 0.8 copy-start.11
  23.0 0.8 copy-start.25
  23.9 0.8 copy-start.26
  24.7 0.8 copy-start.27
  25.5 0.8 copy-start.28
  26.3 0.8 copy-start.29
  27.1 0.8 copy-start.30
  29.5 0.8 copy-start.33
  33.4 0.8 copy-start.41
  34.3 1.2 collective-permute-start
  34.4 20.1 %collective-permute-start.6 = (bf16[512,512]{1,0:T(8,128)(2,1)}, bf16[512,512]{1,0:T(8,128)(2,1)S(1)}, u32[]{:S(2)}, u32[]{:S(2)}) collective-permute-start(bf16[512,512]{1,0:T(8,128)(2,1)} %copy-done.41), channel_id=1, source_target_pairs={{0,2},{1,3},{2,0},{3,1},{4,6},{5,7},{6,4},{7,5},{8,10},{9,11},{10,... | collective-permute-start | bytes 1572872 | tf_op jit(solution)/shard_map/ppermute | solution.py:267
  35.6 13.5 %collective-permute-start.1 = (f32[4,512]{1,0:T(4,128)S(1)}, f32[4,512]{1,0:T(4,128)S(1)}, u32[]{:S(2)}, u32[]{:S(2)}) collective-permute-start(f32[4,512]{1,0:T(4,128)S(1)} %bitcast.66), channel_id=1, source_target_pairs={{0,2},{1,3},{2,0},{3,1},{4,6},{5,7},{6,4},{7,5},{8,10},{9,11},{10,... | collective-permute-start | bytes 24584 | tf_op jit(solution)/shard_map/ppermute | solution.py:267
  49.2 5.3 %collective-permute-start.2 = (f32[2,512]{1,0:T(2,128)S(1)}, f32[2,512]{1,0:T(2,128)S(1)}, u32[]{:S(2)}, u32[]{:S(2)}) collective-permute-start(f32[2,512]{1,0:T(2,128)S(1)} %bitcast.67), channel_id=1, source_target_pairs={{0,4},{1,5},{2,6},{3,7},{4,0},{5,1},{6,2},{7,3},{8,12},{9,13},{10,... | collective-permute-start | bytes 12296 | tf_op jit(solution)/shard_map/ppermute | solution.py:267
  54.5 0.8 copy-start.13
  55.3 7.9 %copy-start.1 = (bf16[1056,512]{1,0:T(8,128)(2,1)}, bf16[1056,512]{1,0:T(8,128)(2,1)S(1)}, u32[]{:S(2)}) copy-start(bf16[1056,512]{1,0:T(8,128)(2,1)S(1)} %collective-permute-done.4.refs_7_) | copy-start | bytes 3244036
  55.3 47.9 %collective-permute-start.8 = (bf16[1056,512]{1,0:T(8,128)(2,1)S(1)}, bf16[1056,512]{1,0:T(8,128)(2,1)S(1)}, u32[]{:S(2)}, u32[]{:S(2)}) collective-permute-start(bf16[1056,512]{1,0:T(8,128)(2,1)S(1)} %collective-permute-done.4.refs_7_), channel_id=1, source_target_pairs={{0,2},{1,3},{2,0},{3,1},{4,6},{5,7},{6,4},{7,5},{8,10},{9,11},{10,... | collective-permute-start | bytes 3244040 | tf_op jit(solution)/shard_map/ppermute | solution.py:267
  56.9 48.1 %collective-permute-start.7 = (bf16[1056,512]{1,0:T(8,128)(2,1)}, bf16[1056,512]{1,0:T(8,128)(2,1)S(1)}, u32[]{:S(2)}, u32[]{:S(2)}) collective-permute-start(bf16[1056,512]{1,0:T(8,128)(2,1)} %collective-permute-done.3.refs_8_), channel_id=1, source_target_pairs={{0,4},{1,5},{2,6},{3,7},{4,0},{5,1},{6,2},{7,3},{8,12},{9,13},{10,... | collective-permute-start | bytes 3244040 | tf_op jit(solution)/shard_map/ppermute | solution.py:267
  58.4 46.7 %collective-permute-start.9 = (bf16[1056,512]{1,0:T(8,128)(2,1)}, bf16[1056,512]{1,0:T(8,128)(2,1)S(1)}, u32[]{:S(2)}, u32[]{:S(2)}) collective-permute-start(bf16[1056,512]{1,0:T(8,128)(2,1)} %collective-permute-done.3.refs_8_), channel_id=1, source_target_pairs={{0,2},{1,3},{2,0},{3,1},{4,6},{5,7},{6,4},{7,5},{8,10},{9,11},{10,... | collective-permute-start | bytes 3244040 | tf_op jit(solution)/shard_map/ppermute | solution.py:267
  58.9 37.0 %collective-permute-start.11 = (bf16[512,512]{1,0:T(8,128)(2,1)}, bf16[512,512]{1,0:T(8,128)(2,1)S(1)}, u32[]{:S(2)}, u32[]{:S(2)}) collective-permute-start(bf16[512,512]{1,0:T(8,128)(2,1)} %copy-done.40), channel_id=1, source_target_pairs={{0,12},{1,13},{2,14},{3,15},{4,8},{5,9},{6,10},{7,11},{8,4},{9,5},... | collective-permute-start | bytes 1572872 | tf_op jit(solution)/shard_map/ppermute | solution.py:267
  60.2 42.9 %collective-permute-start.10 = (bf16[512,512]{1,0:T(8,128)(2,1)}, bf16[512,512]{1,0:T(8,128)(2,1)S(1)}, u32[]{:S(2)}, u32[]{:S(2)}) collective-permute-start(bf16[512,512]{1,0:T(8,128)(2,1)} %copy-done.39), channel_id=1, source_target_pairs={{0,8},{1,9},{2,10},{3,11},{4,12},{5,13},{6,14},{7,15},{8,0},{9,1},... | collective-permute-start | bytes 1572872 | tf_op jit(solution)/shard_map/ppermute | solution.py:267
  60.9 46.7 %copy-start.38 = (bf16[512,512]{1,0:T(8,128)(2,1)S(1)}, bf16[512,512]{1,0:T(8,128)(2,1)}, u32[]{:S(2)}) copy-start(bf16[512,512]{1,0:T(8,128)(2,1)} %copy-done.37) | copy-start | bytes 1572868
  60.9 46.7 %copy-start.36 = (bf16[512,512]{1,0:T(8,128)(2,1)S(1)}, bf16[512,512]{1,0:T(8,128)(2,1)}, u32[]{:S(2)}) copy-start(bf16[512,512]{1,0:T(8,128)(2,1)} %copy-done.35) | copy-start | bytes 1572868
  60.9 49.4 %copy-start.34 = (bf16[512,512]{1,0:T(8,128)(2,1)S(1)}, bf16[512,512]{1,0:T(8,128)(2,1)}, u32[]{:S(2)}) copy-start(bf16[512,512]{1,0:T(8,128)(2,1)} %copy-done.33) | copy-start | bytes 1572868
  103.2 31.1 %copy-start.17 = (bf16[512,512]{1,0:T(8,128)(2,1)}, bf16[512,512]{1,0:T(8,128)(2,1)S(1)}, u32[]{:S(2)}) copy-start(bf16[512,512]{1,0:T(8,128)(2,1)S(1)} %collective-permute-done.10.refs_1_) | copy-start | bytes 1572868
  105.1 29.2 %copy-start.42 = (bf16[1056,512]{1,0:T(8,128)(2,1)}, bf16[1056,512]{1,0:T(8,128)(2,1)S(1)}, u32[]{:S(2)}) copy-start(bf16[1056,512]{1,0:T(8,128)(2,1)S(1)} %collective-permute-done.7.refs_9_) | copy-start | bytes 3244036
  105.1 41.8 %collective-permute-start.13 = (bf16[4,1056,512]{2,1,0:T(8,128)(2,1)S(1)}, bf16[4,1056,512]{2,1,0:T(8,128)(2,1)}, u32[]{:S(2)}, u32[]{:S(2)}) collective-permute-start(bf16[4,1056,512]{2,1,0:T(8,128)(2,1)S(1)} %pad_maximum_fusion), channel_id=1, source_target_pairs={{0,1},{1,0},{2,3},{3,2},{4,5},{5,4},{6,7},{7,6},{8,9},{9,8},{10,11... | collective-permute-start | bytes 12976136 | tf_op jit(solution)/shard_map/ppermute | solution.py:267
  105.1 26.9 %collective-permute-start.12 = (bf16[1056,512]{1,0:T(8,128)(2,1)S(1)}, bf16[1056,512]{1,0:T(8,128)(2,1)S(1)}, u32[]{:S(2)}, u32[]{:S(2)}) collective-permute-start(bf16[1056,512]{1,0:T(8,128)(2,1)S(1)} %collective-permute-done.7.refs_9_), channel_id=1, source_target_pairs={{0,2},{1,3},{2,0},{3,1},{4,6},{5,7},{6,4},{7,5},{8,10},{9,11},{10,... | collective-permute-start | bytes 3244040 | tf_op jit(solution)/shard_map/ppermute | solution.py:267
  107.5 26.8 %collective-permute-start.16 = (bf16[512,512]{1,0:T(8,128)(2,1)S(1)}, bf16[512,512]{1,0:T(8,128)(2,1)S(1)}, u32[]{:S(2)}, u32[]{:S(2)}) collective-permute-start(bf16[512,512]{1,0:T(8,128)(2,1)S(1)} %copy-done.38), channel_id=1, source_target_pairs={{0,9},{1,8},{2,11},{3,10},{4,13},{5,12},{6,15},{7,14},{8,1},{9,0},... | collective-permute-start | bytes 1572872 | tf_op jit(solution)/shard_map/ppermute | solution.py:267
  107.5 37.7 %collective-permute-start.15 = (bf16[512,512]{1,0:T(8,128)(2,1)S(1)}, bf16[512,512]{1,0:T(8,128)(2,1)S(1)}, u32[]{:S(2)}, u32[]{:S(2)}) collective-permute-start(bf16[512,512]{1,0:T(8,128)(2,1)S(1)} %copy-done.36), channel_id=1, source_target_pairs={{0,4},{1,5},{2,6},{3,7},{4,0},{5,1},{6,2},{7,3},{8,12},{9,13},{10,... | collective-permute-start | bytes 1572872 | tf_op jit(solution)/shard_map/ppermute | solution.py:267
  110.3 35.7 %collective-permute-start.17 = (bf16[512,512]{1,0:T(8,128)(2,1)S(1)}, bf16[512,512]{1,0:T(8,128)(2,1)S(1)}, u32[]{:S(2)}, u32[]{:S(2)}) collective-permute-start(bf16[512,512]{1,0:T(8,128)(2,1)S(1)} %copy-done.34), channel_id=1, source_target_pairs={{0,13},{1,12},{2,15},{3,14},{4,9},{5,8},{6,11},{7,10},{8,5},{9,4},... | collective-permute-start | bytes 1572872 | tf_op jit(solution)/shard_map/ppermute | solution.py:267
  132.0 14.9 %copy-start.23 = (s32[1024]{0:T(1024)S(1)}, s32[1024]{0:T(1024)}, u32[]{:S(2)}) copy-start(s32[1024]{0:T(1024)} %param.13) | copy-start | bytes 12292
  134.3 0.9 copy-start.19
  145.2 0.8 copy-start.21
  146.1 0.8 copy-start.9
  146.9 24.6 %collective-permute-start.18 = (bf16[4,1056,512]{2,1,0:T(8,128)(2,1)}, bf16[4,1056,512]{2,1,0:T(8,128)(2,1)}, u32[]{:S(2)}, u32[]{:S(2)}) collective-permute-start(bf16[4,1056,512]{2,1,0:T(8,128)(2,1)} %pad_maximum_fusion.1), channel_id=1, source_target_pairs={{0,1},{1,0},{2,3},{3,2},{4,5},{5,4},{6,7},{7,6},{8,9},{9,8},{10,11... | collective-permute-start | bytes 12976136 | tf_op jit(solution)/shard_map/ppermute | solution.py:267
  147.6 14.2 %collective-permute-start.14 = (f32[1,512]{1,0:T(1,128)S(1)}, f32[1,512]{1,0:T(1,128)S(1)}, u32[]{:S(2)}, u32[]{:S(2)}) collective-permute-start(f32[1,512]{1,0:T(1,128)S(1)} %slice_bitcast_fusion), channel_id=1, source_target_pairs={{0,8},{1,9},{2,10},{3,11},{4,12},{5,13},{6,14},{7,15},{8,0},{9,1},... | collective-permute-start | bytes 6152 | tf_op jit(solution)/shard_map/ppermute | solution.py:267
  158.2 36.8 %collective-permute-start.27 = (bf16[512,512]{1,0:T(8,128)(2,1)}, bf16[512,512]{1,0:T(8,128)(2,1)}, u32[]{:S(2)}, u32[]{:S(2)}) collective-permute-start(bf16[512,512]{1,0:T(8,128)(2,1)} %copy-done.32), channel_id=1, source_target_pairs={{0,3},{1,2},{2,1},{3,0},{4,7},{5,6},{6,5},{7,4},{8,11},{9,10},{10,... | collective-permute-start | bytes 1572872 | tf_op jit(solution)/shard_map/ppermute | solution.py:267
  159.0 36.1 %collective-permute-start.26 = (bf16[512,512]{1,0:T(8,128)(2,1)}, bf16[512,512]{1,0:T(8,128)(2,1)}, u32[]{:S(2)}, u32[]{:S(2)}) collective-permute-start(bf16[512,512]{1,0:T(8,128)(2,1)} %copy-done.31), channel_id=1, source_target_pairs={{0,6},{1,7},{2,4},{3,5},{4,2},{5,3},{6,0},{7,1},{8,14},{9,15},{10,... | collective-permute-start | bytes 1572872 | tf_op jit(solution)/shard_map/ppermute | solution.py:267
  159.8 35.3 %collective-permute-start.25 = (bf16[512,512]{1,0:T(8,128)(2,1)}, bf16[512,512]{1,0:T(8,128)(2,1)}, u32[]{:S(2)}, u32[]{:S(2)}) collective-permute-start(bf16[512,512]{1,0:T(8,128)(2,1)} %copy-done.30), channel_id=1, source_target_pairs={{0,14},{1,15},{2,12},{3,13},{4,10},{5,11},{6,8},{7,9},{8,6},{9,7},... | collective-permute-start | bytes 1572872 | tf_op jit(solution)/shard_map/ppermute | solution.py:267
  161.8 68.2 %collective-permute-start.24 = (bf16[512,512]{1,0:T(8,128)(2,1)}, bf16[512,512]{1,0:T(8,128)(2,1)}, u32[]{:S(2)}, u32[]{:S(2)}) collective-permute-start(bf16[512,512]{1,0:T(8,128)(2,1)} %copy-done.29), channel_id=1, source_target_pairs={{0,10},{1,11},{2,8},{3,9},{4,14},{5,15},{6,12},{7,13},{8,2},{9,3},... | collective-permute-start | bytes 1572872 | tf_op jit(solution)/shard_map/ppermute | solution.py:267
  168.0 62.0 %copy-start.2 = (bf16[1056,512]{1,0:T(8,128)(2,1)S(1)}, bf16[1056,512]{1,0:T(8,128)(2,1)}, u32[]{:S(2)}) copy-start(bf16[1056,512]{1,0:T(8,128)(2,1)} %copy-done.1) | copy-start | bytes 3244036
  168.0 62.0 %copy-start.4 = (bf16[1056,512]{1,0:T(8,128)(2,1)S(1)}, bf16[1056,512]{1,0:T(8,128)(2,1)}, u32[]{:S(2)}) copy-start(bf16[1056,512]{1,0:T(8,128)(2,1)} %copy-done.3) | copy-start | bytes 3244036
  168.0 62.0 %copy-start.12 = (bf16[512,512]{1,0:T(8,128)(2,1)S(1)}, bf16[512,512]{1,0:T(8,128)(2,1)}, u32[]{:S(2)}) copy-start(bf16[512,512]{1,0:T(8,128)(2,1)} %copy-done.11) | copy-start | bytes 1572868
  171.5 81.7 %collective-permute-start.23 = (bf16[512,512]{1,0:T(8,128)(2,1)}, bf16[512,512]{1,0:T(8,128)(2,1)S(1)}, u32[]{:S(2)}, u32[]{:S(2)}) collective-permute-start(bf16[512,512]{1,0:T(8,128)(2,1)} %copy-done.28), channel_id=1, source_target_pairs={{0,15},{1,14},{2,13},{3,12},{4,11},{5,10},{6,9},{7,8},{8,7},{9,6},... | collective-permute-start | bytes 1572872 | tf_op jit(solution)/shard_map/ppermute | solution.py:267
  195.0 58.3 %collective-permute-start.22 = (bf16[512,512]{1,0:T(8,128)(2,1)}, bf16[512,512]{1,0:T(8,128)(2,1)S(1)}, u32[]{:S(2)}, u32[]{:S(2)}) collective-permute-start(bf16[512,512]{1,0:T(8,128)(2,1)} %copy-done.27), channel_id=1, source_target_pairs={{0,1},{1,0},{2,3},{3,2},{4,5},{5,4},{6,7},{7,6},{8,9},{9,8},{10,11... | collective-permute-start | bytes 1572872 | tf_op jit(solution)/shard_map/ppermute | solution.py:267
  195.1 58.2 %collective-permute-start.21 = (bf16[512,512]{1,0:T(8,128)(2,1)}, bf16[512,512]{1,0:T(8,128)(2,1)S(1)}, u32[]{:S(2)}, u32[]{:S(2)}) collective-permute-start(bf16[512,512]{1,0:T(8,128)(2,1)} %copy-done.26), channel_id=1, source_target_pairs={{0,7},{1,6},{2,5},{3,4},{4,3},{5,2},{6,1},{7,0},{8,15},{9,14},{10,... | collective-permute-start | bytes 1572872 | tf_op jit(solution)/shard_map/ppermute | solution.py:267
  195.1 58.2 %collective-permute-start.20 = (bf16[512,512]{1,0:T(8,128)(2,1)}, bf16[512,512]{1,0:T(8,128)(2,1)S(1)}, u32[]{:S(2)}, u32[]{:S(2)}) collective-permute-start(bf16[512,512]{1,0:T(8,128)(2,1)} %copy-done.25), channel_id=1, source_target_pairs={{0,5},{1,4},{2,7},{3,6},{4,1},{5,0},{6,3},{7,2},{8,13},{9,12},{10,... | collective-permute-start | bytes 1572872 | tf_op jit(solution)/shard_map/ppermute | solution.py:267
  230.0 32.0 %collective-permute-start.19 = (bf16[512,512]{1,0:T(8,128)(2,1)}, bf16[512,512]{1,0:T(8,128)(2,1)S(1)}, u32[]{:S(2)}, u32[]{:S(2)}) collective-permute-start(bf16[512,512]{1,0:T(8,128)(2,1)} %copy-done.24), channel_id=1, source_target_pairs={{0,11},{1,10},{2,9},{3,8},{4,15},{5,14},{6,13},{7,12},{8,3},{9,2},... | collective-permute-start | bytes 1572872 | tf_op jit(solution)/shard_map/ppermute | solution.py:267
  230.0 1.0 copy-start.14
  231.1 1.0 copy-start.16
  232.1 1.0 copy-start.18
  233.2 1.0 copy-start.20
  234.2 1.0 copy-start.22
  235.2 8.5 %copy-start.10 = (bf16[512,512]{1,0:T(8,128)(2,1)S(1)}, bf16[512,512]{1,0:T(8,128)(2,1)}, u32[]{:S(2)}) copy-start(bf16[512,512]{1,0:T(8,128)(2,1)} %copy-done.9) | copy-start | bytes 1572868
  253.3 8.8 %copy-start.5 = (s32[1024,1]{1,0:T(8,128)S(1)}, s32[1024,1]{1,0:T(8,128)}, u32[]{:S(2)}) copy-start(s32[1024,1]{1,0:T(8,128)} %copy.21.refs_5_) | copy-start | bytes 12292
  253.3 8.8 %copy-start.6 = (bf16[1024,1024]{1,0:T(8,128)(2,1)S(1)}, bf16[1024,1024]{1,0:T(8,128)(2,1)}, u32[]{:S(2)}) copy-start(bf16[1024,1024]{1,0:T(8,128)(2,1)} %refs_6_.1) | copy-start | bytes 6291460
  260.6 1.3 copy-start.7
  (8 other events, 6.3 us)

commit v3 on v2

--- a/solution.py
+++ b/solution.py
@@ -253,13 +253,13 @@
 ROUNDS = (
     ("z2", "z1", "y0", "s1", "w2", "s2", "s4"),
     ("z3", "y1", "y2", "w8", "w12"),
-    ("y3", "cA", "w4", "w9", "w13"),
-    ("cD", "s8", "w3", "w6", "w10", "w14"),
+    ("y3", "cA", "w4", "w10", "w14"),
+    ("cD", "s8", "w3", "w6", "w9", "w13"),
     ("w1", "w5", "w7", "w11", "w15"),
 )
 LINES = {"z1": ("x", 4), "z2": ("x", 8), "z3": ("z2", 4), "y0": ("x", 2), "y1": ("z1", 2), "y2": ("z2", 2), "y3": ("z3", 2)}
 STACKS = {"cA": ("x", "z1", "z2", "y0"), "cD": ("z3", "y1", "y2", "y3")}
-GROUPS = ((0, 8, 12, 4, 9, 2), (13, 10, 14, 6, 3), (5, 7, 1, 15), (11,))
+GROUPS = ((0, 8, 12, 4, 10, 2), (13, 9, 14, 6, 3), (5, 7, 1, 15), (11,))
 
 
 def exchange(x, blocks, sums):

time: 273 us -> 270 us (0.989)
  waiting for transfers between devices: 124 us -> 137 us
  starting transfers between devices: 61.6 us -> 49 us
  local copies, waits for them, and re-layouts: 31 us -> 27 us
    ppermute x28, waiting for transfers between devices: 124 us -> 137 us  [swap(): return lax.ppermute(array, 'tensor', [(i, i ^ d) for i in range(16)])]
    ppermute x28, starting transfers between devices: 61.6 us -> 49 us  [swap(): return lax.ppermute(array, 'tensor', [(i, i ^ d) for i in range(16)])]
    unnamed x92 -> x94, local copies, waits for them, and re-layouts: 28 us -> 25.5 us
  transfers between devices with their start and end apart: 28 -> 28, of which waited for: 11 -> 11; matrix products, arithmetic and copies ran while one was open for 5% -> 4% of each run, Pallas kernels for 12% -> 12%
where the time goes in v3:
time: 270 us; the launch traced here: 269 us
  waiting for transfers between devices  137 us (51%)
  starting transfers between devices  49 us (18%)
  Pallas kernels  42.2 us (16%)
  local copies, waits for them, and re-layouts  27 us (10%)
  other arithmetic  12.6 us (5%)
    ppermute x28, waiting for transfers between devices, swap(): return lax.ppermute(array, 'tensor', [(i, i ^ d) for i in range(16)])  137 us
    ppermute x28, starting transfers between devices, swap(): return lax.ppermute(array, 'tensor', [(i, i ^ d) for i in range(16)])  49 us
    pallas_call x4, Pallas kernels, merge(): pl.pallas_call(functools.partial(merge_kernel, plan), out_shape=[jax.Shap...  35.5 us
    unnamed x94, local copies, waits for them, and re-layouts  25.5 us
    another operation x3, other arithmetic, payload(): return (jnp.stack([got[k] for k in STACKS[name]]), 1)  7.02 us
    pallas_call x1, Pallas kernels, cut(): pl.pallas_call(cut_kernel, out_shape=[jax.ShapeDtypeStruct((rows, width),...  6.74 us
  transfers between devices with their start and end apart: 28, of which 11 were waited for; matrix products, arithmetic and copies ran while one was open for 4% of the time, Pallas kernels for 12%

profile of v3, /device:TPU:0, one launch (start us, length us, event | category | flops | bytes accessed | tf_op | source)
XLA Modules:
  0.0 269.1 jit_solution(12589797292190676819)
XLA Ops:
  0.6 2.4 fusion.7
  3.1 4.0 %collective-permute-start.3 = (bf16[1056,512]{1,0:T(8,128)(2,1)S(1)}, bf16[1056,512]{1,0:T(8,128)(2,1)}, u32[]{:S(2)}, u32[]{:S(2)}) collective-permute-start(bf16[1056,512]{1,0:T(8,128)(2,1)S(1)} %get-tuple-element.89.refs_6_), channel_id=1, source_target_pairs={{0,8},{1,9},{2,10},{3,11},{4,12},{5,13},{6,14},{7,15},{8,0},{9,1},... | collective-permute-start | bytes 3244040 | tf_op jit(solution)/shard_map/ppermute | solution.py:267
  7.1 1.6 collective-permute-start.4
  8.7 1.5 collective-permute-start.5
  10.4 3.4 %copy-done = bf16[512,8192]{1,0:T(8,128)(2,1)S(1)} copy-done((bf16[512,8192]{1,0:T(8,128)(2,1)S(1)}, bf16[512,8192]{1,0:T(8,128)(2,1)}, u32[]{:S(2)}) %copy-start) | copy-done | bytes 8388632
  13.7 6.7 %shard_map.95 = (bf16[512,512]{1,0:T(8,128)(2,1)S(1)}, bf16[512,512]{1,0:T(8,128)(2,1)S(1)}, bf16[512,512]{1,0:T(8,128)(2,1)S(1)}, bf16[512,512]{1,0:T(8,128)(2,...) custom-call(s32[1]{0:T(128)} %bitcast.me_ref, ...), custom_call_target="tpu_custom_call" | custom-call | flops 16777216 | bytes 16777216 | tf_op jit(solution)/shard_map/pallas_call | solution.py:68
  20.5 0.8 copy-done.11
  21.3 0.8 copy-done.13
  22.1 0.8 copy-done.14
  22.9 0.8 copy-done.15
  23.7 0.8 copy-done.16
  24.5 0.8 copy-done.17
  25.3 0.8 copy-done.19
  26.1 0.8 copy-done.20
  26.9 0.8 copy-done.23
  27.7 0.8 copy-done.24
  28.5 0.8 copy-done.33
  29.3 0.8 copy-done.35
  30.1 0.8 copy-done.37
  30.9 0.8 copy-done.39
  31.7 0.8 copy-done.40
  32.5 0.8 copy-done.41
  34.0 0.6 collective-permute-done
  34.6 1.0 collective-permute-start.1
  35.6 12.5 %collective-permute-done.1 = f32[4,512]{1,0:T(4,128)S(1)} collective-permute-done((f32[4,512]{1,0:T(4,128)S(1)}, f32[4,512]{1,0:T(4,128)S(1)}, u32[]{:S(2)}, u32[]{:S(2)}) %collective-permute-start.1) | collective-permute-done | bytes 8224 | tf_op jit(solution)/shard_map/ppermute | solution.py:267
  48.7 5.8 %collective-permute-done.2 = f32[2,512]{1,0:T(2,128)S(1)} collective-permute-done((f32[2,512]{1,0:T(2,128)S(1)}, f32[2,512]{1,0:T(2,128)S(1)}, u32[]{:S(2)}, u32[]{:S(2)}) %collective-permute-start.2) | collective-permute-done | bytes 4128 | tf_op jit(solution)/shard_map/ppermute | solution.py:267
  54.6 1.6 collective-permute-start.8
  56.2 1.4 collective-permute-start.7
  58.2 1.8 collective-permute-start.11
  60.6 2.3 pad_maximum_fusion
  62.9 32.8 %collective-permute-done.11.refs_2_ = bf16[512,512]{1,0:T(8,128)(2,1)S(1)} collective-permute-done((bf16[512,512]{1,0:T(8,128)(2,1)}, bf16[512,512]{1,0:T(8,128)(2,1)S(1)}, u32[]{:S(2)}, u32[]{:S(2)}) %collective-permute-start.11) | collective-permute-done | bytes 524320 | tf_op jit(solution)/shard_map/ppermute | solution.py:267
  95.6 6.8 %collective-permute-done.10.refs_1_ = bf16[512,512]{1,0:T(8,128)(2,1)S(1)} collective-permute-done((bf16[512,512]{1,0:T(8,128)(2,1)}, bf16[512,512]{1,0:T(8,128)(2,1)S(1)}, u32[]{:S(2)}, u32[]{:S(2)}) %collective-permute-start.10) | collective-permute-done | bytes 524320 | tf_op jit(solution)/shard_map/ppermute | solution.py:267
  102.5 1.9 collective-permute-done.7.refs_9_
  104.4 3.0 %collective-permute-start.12 = (bf16[1056,512]{1,0:T(8,128)(2,1)S(1)}, bf16[1056,512]{1,0:T(8,128)(2,1)S(1)}, u32[]{:S(2)}, u32[]{:S(2)}) collective-permute-start(bf16[1056,512]{1,0:T(8,128)(2,1)S(1)} %collective-permute-done.7.refs_9_), channel_id=1, source_target_pairs={{0,2},{1,3},{2,0},{3,1},{4,6},{5,7},{6,4},{7,5},{8,10},{9,11},{10,... | collective-permute-start | bytes 3244040 | tf_op jit(solution)/shard_map/ppermute | solution.py:267
  107.4 3.1 %collective-permute-start.15 = (bf16[512,512]{1,0:T(8,128)(2,1)S(1)}, bf16[512,512]{1,0:T(8,128)(2,1)S(1)}, u32[]{:S(2)}, u32[]{:S(2)}) collective-permute-start(bf16[512,512]{1,0:T(8,128)(2,1)S(1)} %copy-done.36), channel_id=1, source_target_pairs={{0,4},{1,5},{2,6},{3,7},{4,0},{5,1},{6,2},{7,3},{8,12},{9,13},{10,... | collective-permute-start | bytes 1572872 | tf_op jit(solution)/shard_map/ppermute | solution.py:267
  110.6 2.1 collective-permute-start.17
  112.7 41.6 %collective-permute-done.12.refs_6_ = bf16[1056,512]{1,0:T(8,128)(2,1)S(1)} collective-permute-done((bf16[1056,512]{1,0:T(8,128)(2,1)S(1)}, bf16[1056,512]{1,0:T(8,128)(2,1)S(1)}, u32[]{:S(2)}, u32[]{:S(2)}) %collective-permute-start.12) | collective-permute-done | bytes 1081376 | tf_op jit(solution)/shard_map/ppermute | solution.py:267
  154.4 2.3 pad_maximum_fusion.1
  156.7 0.8 copy-done.29
  157.5 0.8 copy-done.31
  159.3 1.9 collective-permute-start.27
  161.2 2.8 %collective-permute-start.26 = (bf16[512,512]{1,0:T(8,128)(2,1)}, bf16[512,512]{1,0:T(8,128)(2,1)}, u32[]{:S(2)}, u32[]{:S(2)}) collective-permute-start(bf16[512,512]{1,0:T(8,128)(2,1)} %copy-done.23), channel_id=1, source_target_pairs={{0,6},{1,7},{2,4},{3,5},{4,2},{5,3},{6,0},{7,1},{8,14},{9,15},{10,... | collective-permute-start | bytes 1572872 | tf_op jit(solution)/shard_map/ppermute | solution.py:267
  164.0 2.1 collective-permute-start.24
  166.2 3.1 %fusion = (f32[1024,64]{1,0:T(8,128)}, f32[1024,64]{1,0:T(8,128)}, f32[1024,64]{1,0:T(8,128)}) fusion(f32[64]{0:T(128)S(1)} %negate_power_fusion, f32[1024]{0:T(1024)S(1)} %fusion.5), kind=kLoop, calls=%fused_computation.7 | loop fusion | flops 131072 | bytes 790784 | tf_op jit(solution)/shard_map/neg | solution.py:34
  169.6 0.9 dynamic_slice.7
  170.5 1.9 pad_maximum_fusion.3
  172.4 2.4 collective-permute-start.23
  174.8 2.5 collective-permute-done.27.refs_4_
  177.3 0.6 collective-permute-start.22
  177.9 8.4 %collective-permute-done.26.refs_3_ = bf16[512,512]{1,0:T(8,128)(2,1)} collective-permute-done((bf16[512,512]{1,0:T(8,128)(2,1)}, bf16[512,512]{1,0:T(8,128)(2,1)}, u32[]{:S(2)}, u32[]{:S(2)}) %collective-permute-start.26) | collective-permute-done | bytes 524320 | tf_op jit(solution)/shard_map/ppermute | solution.py:267
  186.3 3.0 %collective-permute-start.21 = (bf16[512,512]{1,0:T(8,128)(2,1)}, bf16[512,512]{1,0:T(8,128)(2,1)S(1)}, u32[]{:S(2)}, u32[]{:S(2)}) collective-permute-start(bf16[512,512]{1,0:T(8,128)(2,1)} %copy-done.14), channel_id=1, source_target_pairs={{0,7},{1,6},{2,5},{3,4},{4,3},{5,2},{6,1},{7,0},{8,15},{9,14},{10,... | collective-permute-start | bytes 1572872 | tf_op jit(solution)/shard_map/ppermute | solution.py:267
  189.3 23.8 %collective-permute-done.25.refs_1_ = bf16[512,512]{1,0:T(8,128)(2,1)} collective-permute-done((bf16[512,512]{1,0:T(8,128)(2,1)}, bf16[512,512]{1,0:T(8,128)(2,1)}, u32[]{:S(2)}, u32[]{:S(2)}) %collective-permute-start.25) | collective-permute-done | bytes 524320 | tf_op jit(solution)/shard_map/ppermute | solution.py:267
  213.1 12.4 %collective-permute-start.19 = (bf16[512,512]{1,0:T(8,128)(2,1)S(1)}, bf16[512,512]{1,0:T(8,128)(2,1)S(1)}, u32[]{:S(2)}, u32[]{:S(2)}) collective-permute-start(bf16[512,512]{1,0:T(8,128)(2,1)S(1)} %copy-done.12), channel_id=1, source_target_pairs={{0,11},{1,10},{2,9},{3,8},{4,15},{5,14},{6,13},{7,12},{8,3},{9,2},... | collective-permute-start | bytes 1572872 | tf_op jit(solution)/shard_map/ppermute | solution.py:267
  225.6 1.0 copy-done.18
  226.6 1.0 copy-done.22
  227.7 1.0 copy-done.26
  228.7 1.0 copy-done.28
  229.8 1.0 copy-done.30
  230.8 1.0 copy-done.32
  231.8 8.5 %shard_map.96 = (f32[8192,512]{1,0:T(8,128)}, f32[1024,512]{1,0:T(8,128)}) custom-call(s32[1]{0:T(128)} %bitcast.me_ref, bf16[32,512]{1,0:T(8,128)(2,1)S(1)} %constant_dynamic-slice_fusion.b_ref, f32[1,512]{1,0:T(1,128)S(1)} %bitcast.58, f32[1,512]{1,0:T(1,128)S(1)} %fusion.6.total_ref, bf16[512,512]{1,0:T(8,128)(2,1)S(1)} %copy-done.18, ...), custom_call_target="tpu_custom_call" | custom-call | flops 3221225472 | bytes 15728640 | tf_op jit(solution)/shard_map/pallas_call | solution.py:228
  240.3 9.7 %shard_map.97 = (f32[8192,512]{1,0:T(8,128)}, f32[1024,512]{1,0:T(8,128)}) custom-call(s32[1]{0:T(128)} %bitcast.me_ref, bf16[32,512]{1,0:T(8,128)(2,1)S(1)} %constant_dynamic-slice_fusion.b_ref, f32[1,512]{1,0:T(1,128)S(1)} %bitcast.59, f32[1,512]{1,0:T(1,128)S(1)} %fusion.6.total_ref, ...), custom_call_target="tpu_custom_call", output_to_operand_aliasing={{0}: (14, {})} | custom-call | flops 2684354560 | bytes 13107200 | tf_op jit(solution)/shard_map/pallas_call | solution.py:228
  250.0 7.3 %shard_map.98 = (f32[8192,512]{1,0:T(8,128)}, f32[1024,512]{1,0:T(8,128)S(1)}) custom-call(s32[1]{0:T(128)} %bitcast.me_ref, bf16[32,512]{1,0:T(8,128)(2,1)S(1)} %constant_dynamic-slice_fusion.b_ref, f32[1,512]{1,0:T(1,128)S(1)} %bitcast.60, f32[1,512]{1,0:T(1,128)S(1)} %fusion.6.total_ref, ...), custom_call_target="tpu_custom_call", output_to_operand_aliasing={{0}: (11, {})} | custom-call | flops 2147483648 | bytes 10485760 | tf_op jit(solution)/shard_map/pallas_call | solution.py:228
  257.3 1.3 copy-done.2
  258.9 10.1 %shard_map.99 = (f32[8192,512]{1,0:T(8,128)}, bf16[1024,512]{1,0:T(8,128)(2,1)}) custom-call(s32[1]{0:T(128)} %bitcast.me_ref, bf16[32,512]{1,0:T(8,128)(2,1)S(1)} %constant_dynamic-slice_fusion.b_ref, f32[1,512]{1,0:T(1,128)S(1)} %bitcast.61, f32[1,512]{1,0:T(1,128)S(1)} %fusion.6.total_ref, ...), custom_call_target="tpu_custom_call", output_to_operand_aliasing={{0}: (13, {})} | custom-call | flops 536870912 | bytes 2621440 | tf_op jit(solution)/shard_map/pallas_call | solution.py:228
  (118 shorter events, 4.0 us)
Async XLA Ops:
  0.6 9.6 %copy-start.44 = (bf16[512,32]{0,1:T(8,128)(2,1)S(1)}, bf16[512,32]{0,1:T(8,128)(2,1)}, u32[]{:S(2)}) copy-start(bf16[512,32]{0,1:T(8,128)(2,1)} %param.10) | copy-start | bytes 98308
  0.6 9.7 %copy-start.7 = (bf16[32,8192]{1,0:T(8,128)(2,1)S(1)}, bf16[32,8192]{1,0:T(8,128)(2,1)}, u32[]{:S(2)}) copy-start(bf16[32,8192]{1,0:T(8,128)(2,1)} %b_ref.1) | copy-start | bytes 1572868
  3.1 17.4 %copy-start.5 = (bf16[1056,512]{1,0:T(8,128)(2,1)}, bf16[1056,512]{1,0:T(8,128)(2,1)S(1)}, u32[]{:S(2)}) copy-start(bf16[1056,512]{1,0:T(8,128)(2,1)S(1)} %get-tuple-element.89.refs_6_) | copy-start | bytes 3244036
  3.1 51.5 %collective-permute-start.3 = (bf16[1056,512]{1,0:T(8,128)(2,1)S(1)}, bf16[1056,512]{1,0:T(8,128)(2,1)}, u32[]{:S(2)}, u32[]{:S(2)}) collective-permute-start(bf16[1056,512]{1,0:T(8,128)(2,1)S(1)} %get-tuple-element.89.refs_6_), channel_id=1, source_target_pairs={{0,8},{1,9},{2,10},{3,11},{4,12},{5,13},{6,14},{7,15},{8,0},{9,1},... | collective-permute-start | bytes 3244040 | tf_op jit(solution)/shard_map/ppermute | solution.py:267
  7.1 47.4 %collective-permute-start.4 = (bf16[1056,512]{1,0:T(8,128)(2,1)S(1)}, bf16[1056,512]{1,0:T(8,128)(2,1)S(1)}, u32[]{:S(2)}, u32[]{:S(2)}) collective-permute-start(bf16[1056,512]{1,0:T(8,128)(2,1)S(1)} %get-tuple-element.89.refs_6_), channel_id=1, source_target_pairs={{0,4},{1,5},{2,6},{3,7},{4,0},{5,1},{6,2},{7,3},{8,12},{9,13},{10,... | collective-permute-start | bytes 3244040 | tf_op jit(solution)/shard_map/ppermute | solution.py:267
  8.7 45.9 %collective-permute-start.5 = (bf16[1056,512]{1,0:T(8,128)(2,1)S(1)}, bf16[1056,512]{1,0:T(8,128)(2,1)}, u32[]{:S(2)}, u32[]{:S(2)}) collective-permute-start(bf16[1056,512]{1,0:T(8,128)(2,1)S(1)} %get-tuple-element.89.refs_6_), channel_id=1, source_target_pairs={{0,2},{1,3},{2,0},{3,1},{4,6},{5,7},{6,4},{7,5},{8,10},{9,11},{10,... | collective-permute-start | bytes 3244040 | tf_op jit(solution)/shard_map/ppermute | solution.py:267
  10.4 3.4 %copy-start = (bf16[512,8192]{1,0:T(8,128)(2,1)S(1)}, bf16[512,8192]{1,0:T(8,128)(2,1)}, u32[]{:S(2)}) copy-start(bf16[512,8192]{1,0:T(8,128)(2,1)} %w_ref.1) | copy-start | bytes 25165828
  21.3 0.8 copy-start.13
  23.7 0.8 copy-start.16
  24.5 0.8 copy-start.17
  26.1 0.8 copy-start.20
  27.7 0.8 copy-start.24
  30.1 0.8 copy-start.37
  30.9 0.8 copy-start.39
  33.3 1.2 collective-permute-start
  33.4 21.1 %collective-permute-start.6 = (bf16[512,512]{1,0:T(8,128)(2,1)}, bf16[512,512]{1,0:T(8,128)(2,1)S(1)}, u32[]{:S(2)}, u32[]{:S(2)}) collective-permute-start(bf16[512,512]{1,0:T(8,128)(2,1)} %copy-done.41), channel_id=1, source_target_pairs={{0,2},{1,3},{2,0},{3,1},{4,6},{5,7},{6,4},{7,5},{8,10},{9,11},{10,... | collective-permute-start | bytes 1572872 | tf_op jit(solution)/shard_map/ppermute | solution.py:267
  34.6 13.5 %collective-permute-start.1 = (f32[4,512]{1,0:T(4,128)S(1)}, f32[4,512]{1,0:T(4,128)S(1)}, u32[]{:S(2)}, u32[]{:S(2)}) collective-permute-start(f32[4,512]{1,0:T(4,128)S(1)} %bitcast.66), channel_id=1, source_target_pairs={{0,2},{1,3},{2,0},{3,1},{4,6},{5,7},{6,4},{7,5},{8,10},{9,11},{10,... | collective-permute-start | bytes 24584 | tf_op jit(solution)/shard_map/ppermute | solution.py:267
  48.2 6.3 %collective-permute-start.2 = (f32[2,512]{1,0:T(2,128)S(1)}, f32[2,512]{1,0:T(2,128)S(1)}, u32[]{:S(2)}, u32[]{:S(2)}) collective-permute-start(f32[2,512]{1,0:T(2,128)S(1)} %bitcast.67), channel_id=1, source_target_pairs={{0,4},{1,5},{2,6},{3,7},{4,0},{5,1},{6,2},{7,3},{8,12},{9,13},{10,... | collective-permute-start | bytes 12296 | tf_op jit(solution)/shard_map/ppermute | solution.py:267
  54.5 8.3 %copy-start.21 = (bf16[512,512]{1,0:T(8,128)(2,1)}, bf16[512,512]{1,0:T(8,128)(2,1)S(1)}, u32[]{:S(2)}) copy-start(bf16[512,512]{1,0:T(8,128)(2,1)S(1)} %collective-permute-done.6.refs_5_) | copy-start | bytes 1572868
  54.6 8.3 %copy-start.3 = (bf16[1056,512]{1,0:T(8,128)(2,1)}, bf16[1056,512]{1,0:T(8,128)(2,1)S(1)}, u32[]{:S(2)}) copy-start(bf16[1056,512]{1,0:T(8,128)(2,1)S(1)} %collective-permute-done.4.refs_7_) | copy-start | bytes 3244036
  54.6 47.9 %collective-permute-start.8 = (bf16[1056,512]{1,0:T(8,128)(2,1)S(1)}, bf16[1056,512]{1,0:T(8,128)(2,1)S(1)}, u32[]{:S(2)}, u32[]{:S(2)}) collective-permute-start(bf16[1056,512]{1,0:T(8,128)(2,1)S(1)} %collective-permute-done.4.refs_7_), channel_id=1, source_target_pairs={{0,2},{1,3},{2,0},{3,1},{4,6},{5,7},{6,4},{7,5},{8,10},{9,11},{10,... | collective-permute-start | bytes 3244040 | tf_op jit(solution)/shard_map/ppermute | solution.py:267
  56.2 48.1 %collective-permute-start.7 = (bf16[1056,512]{1,0:T(8,128)(2,1)}, bf16[1056,512]{1,0:T(8,128)(2,1)S(1)}, u32[]{:S(2)}, u32[]{:S(2)}) collective-permute-start(bf16[1056,512]{1,0:T(8,128)(2,1)} %collective-permute-done.3.refs_8_), channel_id=1, source_target_pairs={{0,4},{1,5},{2,6},{3,7},{4,0},{5,1},{6,2},{7,3},{8,12},{9,13},{10,... | collective-permute-start | bytes 3244040 | tf_op jit(solution)/shard_map/ppermute | solution.py:267
  57.7 46.7 %collective-permute-start.9 = (bf16[1056,512]{1,0:T(8,128)(2,1)}, bf16[1056,512]{1,0:T(8,128)(2,1)S(1)}, u32[]{:S(2)}, u32[]{:S(2)}) collective-permute-start(bf16[1056,512]{1,0:T(8,128)(2,1)} %collective-permute-done.3.refs_8_), channel_id=1, source_target_pairs={{0,2},{1,3},{2,0},{3,1},{4,6},{5,7},{6,4},{7,5},{8,10},{9,11},{10,... | collective-permute-start | bytes 3244040 | tf_op jit(solution)/shard_map/ppermute | solution.py:267
  58.2 37.5 %collective-permute-start.11 = (bf16[512,512]{1,0:T(8,128)(2,1)}, bf16[512,512]{1,0:T(8,128)(2,1)S(1)}, u32[]{:S(2)}, u32[]{:S(2)}) collective-permute-start(bf16[512,512]{1,0:T(8,128)(2,1)} %copy-done.40), channel_id=1, source_target_pairs={{0,12},{1,13},{2,14},{3,15},{4,8},{5,9},{6,10},{7,11},{8,4},{9,5},... | collective-permute-start | bytes 1572872 | tf_op jit(solution)/shard_map/ppermute | solution.py:267
  60.0 42.5 %collective-permute-start.10 = (bf16[512,512]{1,0:T(8,128)(2,1)}, bf16[512,512]{1,0:T(8,128)(2,1)S(1)}, u32[]{:S(2)}, u32[]{:S(2)}) collective-permute-start(bf16[512,512]{1,0:T(8,128)(2,1)} %copy-done.39), channel_id=1, source_target_pairs={{0,8},{1,9},{2,10},{3,11},{4,12},{5,13},{6,14},{7,15},{8,0},{9,1},... | collective-permute-start | bytes 1572872 | tf_op jit(solution)/shard_map/ppermute | solution.py:267
  60.6 46.9 %copy-start.38 = (bf16[512,512]{1,0:T(8,128)(2,1)S(1)}, bf16[512,512]{1,0:T(8,128)(2,1)}, u32[]{:S(2)}) copy-start(bf16[512,512]{1,0:T(8,128)(2,1)} %copy-done.37) | copy-start | bytes 1572868
  60.6 46.9 %copy-start.36 = (bf16[512,512]{1,0:T(8,128)(2,1)S(1)}, bf16[512,512]{1,0:T(8,128)(2,1)}, u32[]{:S(2)}) copy-start(bf16[512,512]{1,0:T(8,128)(2,1)} %copy-done.35) | copy-start | bytes 1572868
  60.6 50.0 %copy-start.34 = (bf16[512,512]{1,0:T(8,128)(2,1)S(1)}, bf16[512,512]{1,0:T(8,128)(2,1)}, u32[]{:S(2)}) copy-start(bf16[512,512]{1,0:T(8,128)(2,1)} %copy-done.33) | copy-start | bytes 1572868
  95.6 61.0 %copy-start.25 = (bf16[512,512]{1,0:T(8,128)(2,1)}, bf16[512,512]{1,0:T(8,128)(2,1)S(1)}, u32[]{:S(2)}) copy-start(bf16[512,512]{1,0:T(8,128)(2,1)S(1)} %collective-permute-done.11.refs_2_) | copy-start | bytes 1572868
  102.5 54.2 %copy-start.27 = (bf16[512,512]{1,0:T(8,128)(2,1)}, bf16[512,512]{1,0:T(8,128)(2,1)S(1)}, u32[]{:S(2)}) copy-start(bf16[512,512]{1,0:T(8,128)(2,1)S(1)} %collective-permute-done.10.refs_1_) | copy-start | bytes 1572868
  104.4 52.3 %copy-start.42 = (bf16[1056,512]{1,0:T(8,128)(2,1)}, bf16[1056,512]{1,0:T(8,128)(2,1)S(1)}, u32[]{:S(2)}) copy-start(bf16[1056,512]{1,0:T(8,128)(2,1)S(1)} %collective-permute-done.7.refs_9_) | copy-start | bytes 3244036
  104.4 52.3 %copy-start.43 = (bf16[1056,512]{1,0:T(8,128)(2,1)}, bf16[1056,512]{1,0:T(8,128)(2,1)S(1)}, u32[]{:S(2)}) copy-start(bf16[1056,512]{1,0:T(8,128)(2,1)S(1)} %collective-permute-done.9.refs_11_) | copy-start | bytes 3244036
  104.4 54.0 %collective-permute-start.13 = (bf16[4,1056,512]{2,1,0:T(8,128)(2,1)S(1)}, bf16[4,1056,512]{2,1,0:T(8,128)(2,1)}, u32[]{:S(2)}, u32[]{:S(2)}) collective-permute-start(bf16[4,1056,512]{2,1,0:T(8,128)(2,1)S(1)} %pad_maximum_fusion), channel_id=1, source_target_pairs={{0,1},{1,0},{2,3},{3,2},{4,5},{5,4},{6,7},{7,6},{8,9},{9,8},{10,11... | collective-permute-start | bytes 12976136 | tf_op jit(solution)/shard_map/ppermute | solution.py:267
  104.4 49.9 %collective-permute-start.12 = (bf16[1056,512]{1,0:T(8,128)(2,1)S(1)}, bf16[1056,512]{1,0:T(8,128)(2,1)S(1)}, u32[]{:S(2)}, u32[]{:S(2)}) collective-permute-start(bf16[1056,512]{1,0:T(8,128)(2,1)S(1)} %collective-permute-done.7.refs_9_), channel_id=1, source_target_pairs={{0,2},{1,3},{2,0},{3,1},{4,6},{5,7},{6,4},{7,5},{8,10},{9,11},{10,... | collective-permute-start | bytes 3244040 | tf_op jit(solution)/shard_map/ppermute | solution.py:267
  107.4 49.3 %collective-permute-start.16 = (bf16[512,512]{1,0:T(8,128)(2,1)S(1)}, bf16[512,512]{1,0:T(8,128)(2,1)S(1)}, u32[]{:S(2)}, u32[]{:S(2)}) collective-permute-start(bf16[512,512]{1,0:T(8,128)(2,1)S(1)} %copy-done.38), channel_id=1, source_target_pairs={{0,10},{1,11},{2,8},{3,9},{4,14},{5,15},{6,12},{7,13},{8,2},{9,3},... | collective-permute-start | bytes 1572872 | tf_op jit(solution)/shard_map/ppermute | solution.py:267
  107.4 50.1 %collective-permute-start.15 = (bf16[512,512]{1,0:T(8,128)(2,1)S(1)}, bf16[512,512]{1,0:T(8,128)(2,1)S(1)}, u32[]{:S(2)}, u32[]{:S(2)}) collective-permute-start(bf16[512,512]{1,0:T(8,128)(2,1)S(1)} %copy-done.36), channel_id=1, source_target_pairs={{0,4},{1,5},{2,6},{3,7},{4,0},{5,1},{6,2},{7,3},{8,12},{9,13},{10,... | collective-permute-start | bytes 1572872 | tf_op jit(solution)/shard_map/ppermute | solution.py:267
  110.6 47.8 %collective-permute-start.17 = (bf16[512,512]{1,0:T(8,128)(2,1)S(1)}, bf16[512,512]{1,0:T(8,128)(2,1)S(1)}, u32[]{:S(2)}, u32[]{:S(2)}) collective-permute-start(bf16[512,512]{1,0:T(8,128)(2,1)S(1)} %copy-done.34), channel_id=1, source_target_pairs={{0,14},{1,15},{2,12},{3,13},{4,10},{5,11},{6,8},{7,9},{8,6},{9,7},... | collective-permute-start | bytes 1572872 | tf_op jit(solution)/shard_map/ppermute | solution.py:267
  154.4 4.1 %copy-start.10 = (s32[1024]{0:T(1024)S(1)}, s32[1024]{0:T(1024)}, u32[]{:S(2)}) copy-start(s32[1024]{0:T(1024)} %param.13) | copy-start | bytes 12292
  156.7 0.8 copy-start.29
  157.5 0.8 copy-start.31
  158.4 10.9 %copy-start.8 = (bf16[512,512]{1,0:T(8,128)(2,1)}, bf16[512,512]{1,0:T(8,128)(2,1)S(1)}, u32[]{:S(2)}) copy-start(bf16[512,512]{1,0:T(8,128)(2,1)S(1)} %collective-permute-done.17.refs_2_) | copy-start | bytes 1572868
  158.4 14.0 %collective-permute-start.18 = (bf16[4,1056,512]{2,1,0:T(8,128)(2,1)}, bf16[4,1056,512]{2,1,0:T(8,128)(2,1)}, u32[]{:S(2)}, u32[]{:S(2)}) collective-permute-start(bf16[4,1056,512]{2,1,0:T(8,128)(2,1)} %pad_maximum_fusion.1), channel_id=1, source_target_pairs={{0,1},{1,0},{2,3},{3,2},{4,5},{5,4},{6,7},{7,6},{8,9},{9,8},{10,11... | collective-permute-start | bytes 12976136 | tf_op jit(solution)/shard_map/ppermute | solution.py:267
  159.2 4.8 %collective-permute-start.14 = (f32[1,512]{1,0:T(1,128)S(1)}, f32[1,512]{1,0:T(1,128)S(1)}, u32[]{:S(2)}, u32[]{:S(2)}) collective-permute-start(f32[1,512]{1,0:T(1,128)S(1)} %slice_bitcast_fusion), channel_id=1, source_target_pairs={{0,8},{1,9},{2,10},{3,11},{4,12},{5,13},{6,14},{7,15},{8,0},{9,1},... | collective-permute-start | bytes 6152 | tf_op jit(solution)/shard_map/ppermute | solution.py:267
  159.3 18.0 %collective-permute-start.27 = (bf16[512,512]{1,0:T(8,128)(2,1)}, bf16[512,512]{1,0:T(8,128)(2,1)}, u32[]{:S(2)}, u32[]{:S(2)}) collective-permute-start(bf16[512,512]{1,0:T(8,128)(2,1)} %copy-done.24), channel_id=1, source_target_pairs={{0,3},{1,2},{2,1},{3,0},{4,7},{5,6},{6,5},{7,4},{8,11},{9,10},{10,... | collective-permute-start | bytes 1572872 | tf_op jit(solution)/shard_map/ppermute | solution.py:267
  161.2 25.1 %collective-permute-start.26 = (bf16[512,512]{1,0:T(8,128)(2,1)}, bf16[512,512]{1,0:T(8,128)(2,1)}, u32[]{:S(2)}, u32[]{:S(2)}) collective-permute-start(bf16[512,512]{1,0:T(8,128)(2,1)} %copy-done.23), channel_id=1, source_target_pairs={{0,6},{1,7},{2,4},{3,5},{4,2},{5,3},{6,0},{7,1},{8,14},{9,15},{10,... | collective-permute-start | bytes 1572872 | tf_op jit(solution)/shard_map/ppermute | solution.py:267
  164.0 49.1 %collective-permute-start.25 = (bf16[512,512]{1,0:T(8,128)(2,1)}, bf16[512,512]{1,0:T(8,128)(2,1)}, u32[]{:S(2)}, u32[]{:S(2)}) collective-permute-start(bf16[512,512]{1,0:T(8,128)(2,1)} %copy-done.20), channel_id=1, source_target_pairs={{0,9},{1,8},{2,11},{3,10},{4,13},{5,12},{6,15},{7,14},{8,1},{9,0},... | collective-permute-start | bytes 1572872 | tf_op jit(solution)/shard_map/ppermute | solution.py:267
  164.0 49.1 %collective-permute-start.24 = (bf16[512,512]{1,0:T(8,128)(2,1)}, bf16[512,512]{1,0:T(8,128)(2,1)}, u32[]{:S(2)}, u32[]{:S(2)}) collective-permute-start(bf16[512,512]{1,0:T(8,128)(2,1)} %copy-done.19), channel_id=1, source_target_pairs={{0,13},{1,12},{2,15},{3,14},{4,9},{5,8},{6,11},{7,10},{8,5},{9,4},... | collective-permute-start | bytes 1572872 | tf_op jit(solution)/shard_map/ppermute | solution.py:267
  169.5 43.6 %copy-start.12 = (bf16[512,512]{1,0:T(8,128)(2,1)S(1)}, bf16[512,512]{1,0:T(8,128)(2,1)}, u32[]{:S(2)}) copy-start(bf16[512,512]{1,0:T(8,128)(2,1)} %copy-done.11) | copy-start | bytes 1572868
  169.6 56.0 %copy-start.4 = (bf16[1056,512]{1,0:T(8,128)(2,1)S(1)}, bf16[1056,512]{1,0:T(8,128)(2,1)}, u32[]{:S(2)}) copy-start(bf16[1056,512]{1,0:T(8,128)(2,1)} %copy-done.3) | copy-start | bytes 3244036
  169.6 56.0 %copy-start.6 = (bf16[1056,512]{1,0:T(8,128)(2,1)S(1)}, bf16[1056,512]{1,0:T(8,128)(2,1)}, u32[]{:S(2)}) copy-start(bf16[1056,512]{1,0:T(8,128)(2,1)} %copy-done.5) | copy-start | bytes 3244036
  172.4 77.6 %collective-permute-start.23 = (bf16[512,512]{1,0:T(8,128)(2,1)}, bf16[512,512]{1,0:T(8,128)(2,1)S(1)}, u32[]{:S(2)}, u32[]{:S(2)}) collective-permute-start(bf16[512,512]{1,0:T(8,128)(2,1)} %copy-done.16), channel_id=1, source_target_pairs={{0,15},{1,14},{2,13},{3,12},{4,11},{5,10},{6,9},{7,8},{8,7},{9,6},... | collective-permute-start | bytes 1572872 | tf_op jit(solution)/shard_map/ppermute | solution.py:267
  177.3 72.7 %collective-permute-start.22 = (bf16[512,512]{1,0:T(8,128)(2,1)}, bf16[512,512]{1,0:T(8,128)(2,1)S(1)}, u32[]{:S(2)}, u32[]{:S(2)}) collective-permute-start(bf16[512,512]{1,0:T(8,128)(2,1)} %copy-done.15), channel_id=1, source_target_pairs={{0,1},{1,0},{2,3},{3,2},{4,5},{5,4},{6,7},{7,6},{8,9},{9,8},{10,11... | collective-permute-start | bytes 1572872 | tf_op jit(solution)/shard_map/ppermute | solution.py:267
  186.3 63.7 %collective-permute-start.21 = (bf16[512,512]{1,0:T(8,128)(2,1)}, bf16[512,512]{1,0:T(8,128)(2,1)S(1)}, u32[]{:S(2)}, u32[]{:S(2)}) collective-permute-start(bf16[512,512]{1,0:T(8,128)(2,1)} %copy-done.14), channel_id=1, source_target_pairs={{0,7},{1,6},{2,5},{3,4},{4,3},{5,2},{6,1},{7,0},{8,15},{9,14},{10,... | collective-permute-start | bytes 1572872 | tf_op jit(solution)/shard_map/ppermute | solution.py:267
  213.1 36.9 %collective-permute-start.20 = (bf16[512,512]{1,0:T(8,128)(2,1)}, bf16[512,512]{1,0:T(8,128)(2,1)S(1)}, u32[]{:S(2)}, u32[]{:S(2)}) collective-permute-start(bf16[512,512]{1,0:T(8,128)(2,1)} %copy-done.13), channel_id=1, source_target_pairs={{0,5},{1,4},{2,7},{3,6},{4,1},{5,0},{6,3},{7,2},{8,13},{9,12},{10,... | collective-permute-start | bytes 1572872 | tf_op jit(solution)/shard_map/ppermute | solution.py:267
  213.1 45.7 %collective-permute-start.19 = (bf16[512,512]{1,0:T(8,128)(2,1)S(1)}, bf16[512,512]{1,0:T(8,128)(2,1)S(1)}, u32[]{:S(2)}, u32[]{:S(2)}) collective-permute-start(bf16[512,512]{1,0:T(8,128)(2,1)S(1)} %copy-done.12), channel_id=1, source_target_pairs={{0,11},{1,10},{2,9},{3,8},{4,15},{5,14},{6,13},{7,12},{8,3},{9,2},... | collective-permute-start | bytes 1572872 | tf_op jit(solution)/shard_map/ppermute | solution.py:267
  225.6 1.0 copy-start.18
  226.6 1.0 copy-start.22
  227.7 1.0 copy-start.26
  228.7 1.0 copy-start.28
  229.8 1.0 copy-start.30
  230.8 1.0 copy-start.32
  231.8 8.5 %copy-start.9 = (bf16[512,512]{1,0:T(8,128)(2,1)S(1)}, bf16[512,512]{1,0:T(8,128)(2,1)}, u32[]{:S(2)}) copy-start(bf16[512,512]{1,0:T(8,128)(2,1)} %copy-done.8) | copy-start | bytes 1572868
  250.0 8.8 %copy-start.1 = (bf16[1024,1024]{1,0:T(8,128)(2,1)S(1)}, bf16[1024,1024]{1,0:T(8,128)(2,1)}, u32[]{:S(2)}) copy-start(bf16[1024,1024]{1,0:T(8,128)(2,1)} %refs_6_.1) | copy-start | bytes 6291460
  257.3 1.3 copy-start.2
  (9 other events, 7.1 us)
